TPU v7x, 512 devices: a whole 4x4x16 slice. The times are simulated.
512 devices in a mesh: video: 4 (over x), patch: 32 (over z, y_lo), head: 4 (over y_hi, core).
Axes of the slice: x: 4, y: 4 (y_hi: 2, y_lo: 2; y = y_hi * 2 + y_lo), z: 16, core: 2. Of those that a mesh axis runs over, the one named last changes fastest.
Arguments:
- fresh_q: bfloat16 [24576, 2560], P(('video', 'patch', 'head')), parts along dimension 0, may hold values from -7 to 7
- fresh_k: bfloat16 [24576, 2560], P(('video', 'patch', 'head')), parts along dimension 0, may hold values from -6.375 to 6.375
- fresh_v: bfloat16 [24576, 2560], P(('video', 'patch', 'head')), parts along dimension 0, may hold values from -4 to 4
- stale_k: bfloat16 [24576, 2560], P(('video', 'patch'), 'head'), parts along dimension 0, may hold values from -26 to 26
- stale_v: bfloat16 [24576, 2560], P(('video', 'patch'), 'head'), parts along dimension 0, may hold values from -16 to 16
- scale_exps: int32 [24576, 2], P(('video', 'patch')), parts along dimension 0, may hold values from -2 to 2, as said below
Outputs:
- attended: bfloat16 [24576, 2560], P(('video', 'patch', 'head')), parts along dimension 0
There are 4 independent parts, one for each index of `video`. A program takes and returns all parts, laid end to end along the dimension named above; each array names one. Nothing has to cross between parts.
Inputs may be any that keep to these rules, and one draw needn't show every extreme that they name: `scale_exps`: column 0 is the exponent for the key row, column 1 for the value row.
All inputs are finite; a program needn't handle non-finite values.
Results may differ from a plain program's by a relative error of at most 0.0055.
Values may be sent and summed in bfloat16 or wider, within the bound.
No kernel may reach another device: no remote copies, remote signals or barrier semaphores. Data moves between devices by JAX's collectives and lax.ppermute only.
A program may use at most 128 MiB of HBM per device.

v0:
```python
import math

import jax
import jax.numpy as jnp
from jax import lax
from jax.sharding import PartitionSpec as P

HD = 128


masked_score = -1e30


def block_size(total_rows, upper):
    chosen = 1
    for divisor in range(1, min(total_rows, upper) + 1):
        if total_rows % divisor == 0:
            chosen = divisor
    return chosen


def attend(running, query_heads, key_rows, value_rows, exponents, skip_lower, skip_upper):
    key_count, row_width = key_rows.shape
    head_count = query_heads.shape[1]
    head_size = query_heads.shape[2]
    block_rows = block_size(key_count, 1536)
    block_count = key_count // block_rows
    factor = 1.0 / math.sqrt(head_size)

    def one_block(state, items):
        key_block, value_block, exp_block, offset = items
        key_scale = jnp.exp2(exp_block[:, 0].astype(jnp.float32))
        value_scale = jnp.exp2(exp_block[:, 1].astype(jnp.float32))
        key_full = (key_block.astype(jnp.float32) * key_scale[:, None]).astype(jnp.bfloat16)
        value_full = (value_block.astype(jnp.float32) * value_scale[:, None]).astype(jnp.bfloat16)
        positions = offset + jnp.arange(block_rows, dtype=jnp.int32)
        usable = (positions < skip_lower) | (positions >= skip_upper)
        scores = (
            jnp.einsum(
                "rhd,khd->rhk",
                query_heads,
                key_full.reshape(block_rows, head_count, head_size),
                preferred_element_type=jnp.float32,
            )
            * factor
        )
        scores = jnp.where(usable[None, None, :], scores, masked_score)
        old_max, old_total, old_acc = state
        new_max = jnp.maximum(old_max, jnp.max(scores, axis=-1))
        expon = jnp.where(usable[None, None, :], jnp.exp(scores - new_max[:, :, None]), 0.0)
        shrink = jnp.exp(old_max - new_max)
        new_total = old_total * shrink + jnp.sum(expon, axis=-1)
        product = jnp.einsum(
            "rhk,khd->rhd",
            expon.astype(jnp.bfloat16),
            value_full.reshape(block_rows, head_count, head_size),
            preferred_element_type=jnp.float32,
        )
        new_acc = old_acc * shrink[:, :, None] + product
        return ((new_max, new_total, new_acc), None)

    offsets = block_rows * jnp.arange(block_count, dtype=jnp.int32)
    items = (
        key_rows.reshape(block_count, block_rows, row_width),
        value_rows.reshape(block_count, block_rows, row_width),
        exponents.reshape(block_count, block_rows, 2),
        offsets,
    )
    finished, unused = lax.scan(one_block, running, items)
    return finished


def per_device(fresh_q, fresh_k, fresh_v, stale_k, stale_v, scale_exps):
    head_q, head_k, head_v = (
        lax.all_to_all(fresh_q, "head", split_axis=1, concat_axis=0, tiled=True),
        lax.all_to_all(fresh_k, "head", split_axis=1, concat_axis=0, tiled=True),
        lax.all_to_all(fresh_v, "head", split_axis=1, concat_axis=0, tiled=True),
    )
    query_rows, row_width = head_q.shape
    head_count = row_width // HD
    query_heads = head_q.reshape(query_rows, head_count, HD)
    own_lower = lax.axis_index("patch") * query_rows
    own_upper = own_lower + query_rows
    initial = (
        jnp.full((query_rows, head_count), masked_score, jnp.float32),
        jnp.zeros((query_rows, head_count), jnp.float32),
        jnp.zeros((query_rows, head_count, HD), jnp.float32),
    )
    no_exponent = jnp.zeros((query_rows, 2), jnp.int32)
    all_keys = lax.all_gather(stale_k, "patch", axis=0, tiled=True)
    all_values = lax.all_gather(stale_v, "patch", axis=0, tiled=True)
    all_exps = lax.all_gather(scale_exps, "patch", axis=0, tiled=True)
    finished = attend(
        attend(initial, query_heads, head_k, head_v, no_exponent, 0, 0),
        query_heads,
        all_keys,
        all_values,
        all_exps,
        own_lower,
        own_upper,
    )
    result = finished[2] / finished[1][:, :, None]
    result = result.reshape(query_rows, row_width).astype(jnp.bfloat16)
    return lax.all_to_all(result, "head", split_axis=0, concat_axis=1, tiled=True)


def solution(mesh):
    in_specs = (
        P(("video", "patch", "head"), None),
        P(("video", "patch", "head"), None),
        P(("video", "patch", "head"), None),
        P(("video", "patch"), "head"),
        P(("video", "patch"), "head"),
        P(("video", "patch"), None),
    )
    out_specs = P(("video", "patch", "head"), None)
    return jax.shard_map(
        per_device, mesh=mesh, in_specs=in_specs, out_specs=out_specs, check_vma=False
    )
```

profile of v0, /device:TPU:1, one launch (start us, length us, event | category | flops | bytes accessed | tf_op | source)
XLA Modules:
  0.0 479.1 jit_solution(902022789092675144)
XLA Ops:
  8.0 1.7 copy.77
  9.7 10.2 %all-to-all-start.1 = ((bf16[48,4,640]{2,0,1:T(8,128)(2,1)}), bf16[48,4,640]{2,0,1:T(8,128)(2,1)S(1)}, u32[]{:S(2)}, u32[]{:S(2)}) async-start(bf16[48,4,640]{2,0,1:T(8,128)(2,1)} %bitcast.57), calls=%async_computation.1 | async-start | bytes 491520 | tf_op jit(solution)/shard_map/all_to_all | solution.py:75
  19.9 1.7 copy.78
  21.6 4.8 %all-to-all-done.1 = bf16[48,4,640]{2,0,1:T(8,128)(2,1)S(1)} async-done(((bf16[48,4,640]{2,0,1:T(8,128)(2,1)}), bf16[48,4,640]{2,0,1:T(8,128)(2,1)S(1)}, u32[]{:S(2)}, u32[]{:S(2)}) %all-to-all-start.1) | async-done | bytes 245792 | tf_op jit(solution)/shard_map/all_to_all | solution.py:75
  26.4 4.2 all-to-all-start
  30.6 1.7 copy.76
  32.3 13.2 %all-to-all-done = bf16[48,4,640]{2,0,1:T(8,128)(2,1)S(1)} async-done(((bf16[48,4,640]{2,0,1:T(8,128)(2,1)}), bf16[48,4,640]{2,0,1:T(8,128)(2,1)S(1)}, u32[]{:S(2)}, u32[]{:S(2)}) %all-to-all-start) | async-done | bytes 245792 | tf_op jit(solution)/shard_map/all_to_all | solution.py:76
  45.6 4.6 all-to-all-start.2
  50.2 57.5 %all-gather = s32[32,192,2]{1,2,0:T(2,128)S(1)} all-gather(s32[1,192,2]{1,2,0:T(2,128)} %bitcast.89), channel_id=1, replica_groups=mesh['video'=4,'patch'=32,'head'=4] {'patch'}, dimensions={0}, use_global_device_ids=true | all-gather | bytes 50688 | tf_op jit(solution)/shard_map/all_gather | solution.py:92
  109.7 96.0 %all-gather.4.cloned.1.call-done = bf16[6144,640]{1,0:T(8,128)(2,1)} async-done(((bf16[192,640]{1,0:T(8,128)(2,1)}), bf16[6144,640]{1,0:T(8,128)(2,1)}) %all-gather.4.cloned.1.call-update) | async-done | bytes 7864336 | tf_op jit(solution)/shard_map/all_gather | solution.py:90
  205.8 185.3 %all-gather.6.cloned.1.call-done = bf16[6144,640]{1,0:T(8,128)(2,1)} async-done(((bf16[192,640]{1,0:T(8,128)(2,1)}), bf16[6144,640]{1,0:T(8,128)(2,1)}) %all-gather.6.cloned.1.call-update) | async-done | bytes 7864336 | tf_op jit(solution)/shard_map/all_gather | solution.py:91
  391.0 68.2 %while.2 = (s32[]{:T(128)}, f32[192,5]{0,1:T(8,128)S(1)}, f32[192,5]{0,1:T(8,128)S(1)}, f32[192,5,128]{2,0,1:T(8,128)S(1)}, s32[4]{0:T(128)S(1)}, /*index=5*/s32...) while((s32[]{:T(128)}, f32[192,5]{0,1:T(8,128)S(1)}, ...), condition=%wide.region_5.6_spmd, body=%wide.region_2.5_spmd.sunk | while | flops 780302208 | bytes 46602424 | solution.py:69
  392.4 4.4 constant_dynamic-slice_fusion.5
  396.8 2.7 copy.82
  399.5 4.0 copy.84
  404.8 1.5 fusion.61
  406.3 1.8 fusion.62
  409.4 4.4 constant_dynamic-slice_fusion.5
  413.8 2.7 copy.82
  416.5 4.0 copy.84
  421.8 1.5 fusion.61
  423.4 1.8 fusion.62
  426.5 4.4 constant_dynamic-slice_fusion.5
  430.9 2.7 copy.82
  433.6 4.0 copy.84
  438.9 1.5 fusion.61
  440.4 1.8 fusion.62
  443.5 4.4 constant_dynamic-slice_fusion.5
  447.9 2.7 copy.82
  450.6 4.0 copy.84
  457.5 1.8 fusion.62
  460.0 11.6 %all_to_all.64 = bf16[4,48,640]{2,1,0:T(8,128)(2,1)S(1)} all-to-all(bf16[4,48,640]{2,1,0:T(8,128)(2,1)S(1)} %convert_element_type.66), channel_id=1, replica_groups=mesh['video'=4,'patch'=32,'head'=4] {'head'}, dimensions={0} | all-to-all | bytes 491520 | tf_op jit(solution)/shard_map/all_to_all | solution.py:104
  (66 shorter events, 16.7 us)
Async XLA Ops:
  6.5 199.2 %all-gather.4.cloned.1.call-start = ((), (), s32[]{:S(2)}) async-start(), calls=%async_computation.4 | async-start | bytes 8110080 | tf_op jit(solution)/shard_map/all_gather | solution.py:90
  7.3 383.8 %all-gather.6.cloned.1.call-start = ((), (), s32[]{:S(2)}) async-start(), calls=%async_computation.5 | async-start | bytes 8110080 | tf_op jit(solution)/shard_map/all_gather | solution.py:91
  9.7 16.7 %all-to-all-start.1 = ((bf16[48,4,640]{2,0,1:T(8,128)(2,1)}), bf16[48,4,640]{2,0,1:T(8,128)(2,1)S(1)}, u32[]{:S(2)}, u32[]{:S(2)}) async-start(bf16[48,4,640]{2,0,1:T(8,128)(2,1)} %bitcast.57), calls=%async_computation.1 | async-start | bytes 491520 | tf_op jit(solution)/shard_map/all_to_all | solution.py:75
  26.4 19.2 %all-to-all-start = ((bf16[48,4,640]{2,0,1:T(8,128)(2,1)}), bf16[48,4,640]{2,0,1:T(8,128)(2,1)S(1)}, u32[]{:S(2)}, u32[]{:S(2)}) async-start(bf16[48,4,640]{2,0,1:T(8,128)(2,1)} %bitcast.58), calls=%async_computation | async-start | bytes 491520 | tf_op jit(solution)/shard_map/all_to_all | solution.py:76
  45.6 62.9 %all-to-all-start.2 = ((bf16[48,4,640]{2,0,1:T(8,128)(2,1)}), bf16[48,4,640]{2,0,1:T(8,128)(2,1)S(1)}, u32[]{:S(2)}, u32[]{:S(2)}) async-start(bf16[48,4,640]{2,0,1:T(8,128)(2,1)} %bitcast.56), calls=%async_computation.2 | async-start | bytes 491520 | tf_op jit(solution)/shard_map/all_to_all | solution.py:77
  403.5 2.8 copy-start
  420.5 2.8 copy-start
  437.6 2.8 copy-start
  454.6 2.8 copy-start
Sparse Core Ops, SparseCore 0:
  9.4 196.2 all-gather.3
  207.8 183.1 all-gather.5
where the time goes:
time: 480 us; the launch traced here: 479 us
  waiting for transfers between devices  301 us (63%)
  blocking collectives  69.2 us (14%)
  local copies, waits for them, and re-layouts  54 us (11%)
  starting transfers between devices  19.1 us (4%)
  between operations  13.5 us (3%)
  matrix products  12.9 us (3%)
  other arithmetic  9.27 us (2%)
    all_gather x1, waiting for transfers between devices, per_device(): all_values = lax.all_gather(stale_v, 'patch', axis=0, tiled=True)  185 us
    all_gather x1, waiting for transfers between devices, per_device(): all_keys = lax.all_gather(stale_k, 'patch', axis=0, tiled=True)  96 us
    all_gather x1, blocking collectives, per_device(): all_exps = lax.all_gather(scale_exps, 'patch', axis=0, tiled=True)  57.5 us
    dynamic_slice x24, local copies, waits for them, and re-layouts, attend(): finished, unused = lax.scan(one_block, running, items)  46.7 us
    all_to_all x1, waiting for transfers between devices, per_device(): lax.all_to_all(fresh_k, 'head', split_axis=1, concat_axis=0, tiled=True)  13.2 us
    all_to_all x1, blocking collectives, per_device(): lax.all_to_all(result, 'head', split_axis=0, concat_axis=1, tiled=True)  11.6 us
    all_to_all x1, starting transfers between devices, per_device(): lax.all_to_all(fresh_q, 'head', split_axis=1, concat_axis=0, tiled=True)  10.2 us
  transfers between devices with their start and end apart: 5, of which 4 were waited for; matrix products, arithmetic and copies ran while one was open for 1% of the time, Pallas kernels for 0%

commit v1 on v0

v1 whole, which is shorter than its diff:
```python
import functools
import math

import jax
import jax.numpy as jnp
import numpy as np
from jax import lax
from jax.experimental import pallas as pl
from jax.experimental.pallas import tpu as pltpu
from jax.sharding import Mesh, PartitionSpec as P


HD = 128
LOG2_SCALE = math.log2(math.e) / math.sqrt(HD)
LOWEST = -1e30
SUB = 48
PATCH = 192
PACKED = 64
VMEM_BYTES = 40 * 2**20
VM = pl.BlockSpec(memory_space=pltpu.VMEM)
SM = pl.BlockSpec(memory_space=pltpu.SMEM)
BF16, F32 = jnp.bfloat16, jnp.float32
CHUNKS = ((0, 1), (2, 3))
STEPS_Y = (0, 1, 3, 2)


def call(kernel, name, outs, in_specs):
    return pl.pallas_call(
        kernel,
        out_shape=outs,
        in_specs=in_specs,
        out_specs=[VM] * len(outs),
        compiler_params=pltpu.CompilerParams(vmem_limit_bytes=VMEM_BYTES),
        name=name,
    )


def prepare_kernel(first_ref, k_ref, v_ref, exps_ref, q_ref, fk_ref, fv_ref, *outs):
    rounds, line_ref, q_plane_ref, q_line_ref, fresh_ref = outs[:4], *outs[4:]
    scales = jnp.exp2(exps_ref[...].astype(F32))
    k_scale, v_scale = scales[:, 0:1], scales[:, 1:2]

    def pair(column):
        k = k_ref[:, pl.ds(column, HD)].astype(F32) * k_scale
        v = v_ref[:, pl.ds(column, HD)].astype(F32) * v_scale
        return k.astype(BF16), v.astype(BF16)

    for r in range(4):
        j = (first_ref[0] + r) % 4
        k, v = pair(pl.multiple_of(j * HD, HD))
        rounds[r][:, :HD] = k
        rounds[r][:, HD:] = v
    k, v = pair(4 * HD)
    line_ref[:, :HD] = k
    line_ref[:, HD:] = v
    for g in range(4):
        for j in range(4):
            at = (5 * g + j) * HD
            q_plane_ref[4 * j + g] = q_ref[:, at : at + HD]
        at = (5 * g + 4) * HD
        q_line_ref[g] = q_ref[:, at : at + HD]
        q_line_ref[4 + g] = q_ref[:, at : at + HD]
    width = fk_ref.shape[1]
    fresh_ref[:, :width] = fk_ref[...]
    fresh_ref[:, width:] = fv_ref[...]


def attend_kernel(group, has_state, last, n_kv, *refs):
    spans_ref, q_ref = refs[:2]
    kv_refs = refs[2 : 2 + n_kv]
    rest = refs[2 + n_kv :]
    queries = q_ref[...]
    count = queries.shape[0]
    lanes = lax.broadcasted_iota(jnp.int32, (1, count), 1)
    keys = group * PATCH

    if has_state:
        state = tuple(ref[...] for ref in rest[:3])
        rest = rest[3:]
    else:
        state = (
            jnp.full((1, count), LOWEST, F32),
            jnp.zeros((1, count), F32),
            jnp.zeros((HD, count), F32),
        )
    patch = 0
    for kv_ref in kv_refs:

        def step(i, state, kv_ref=kv_ref, patch=patch):
            top, total, acc = state
            rows = pl.ds(pl.multiple_of(i * keys, keys), keys)
            k, v = kv_ref[rows, :HD], kv_ref[rows, HD:]
            s = lax.dot_general(k, queries, (((1,), (1,)), ((), ())), preferred_element_type=F32)
            blocks, masks = [], []
            new_top = top
            for n in range(group):
                block = s[n * PATCH : (n + 1) * PATCH]
                at = patch + i * group + n
                mask = (lanes >= spans_ref[at, 0]) & (lanes < spans_ref[at, 1])
                block_top = jnp.max(block, axis=0, keepdims=True)
                new_top = jnp.maximum(new_top, jnp.where(mask, LOWEST, block_top))
                blocks.append(block)
                masks.append(mask)
            shift = new_top * LOG2_SCALE
            weights = []
            shrink = jnp.exp2(top * LOG2_SCALE - shift)
            total = total * shrink
            for block, mask in zip(blocks, masks):
                w = jnp.exp2(block * LOG2_SCALE - jnp.where(mask, -LOWEST, shift))
                total = total + jnp.sum(w, axis=0, keepdims=True)
                weights.append(w.astype(BF16))
            w = jnp.concatenate(weights, axis=0)
            acc = acc * shrink + lax.dot_general(
                v, w, (((0,), (0,)), ((), ())), preferred_element_type=F32
            )
            return new_top, total, acc

        steps = kv_ref.shape[0] // keys
        state = lax.fori_loop(0, steps, step, state)
        patch += steps * group

    if not last:
        for ref, value in zip(rest, state):
            ref[...] = value
        return
    (out_ref,) = rest
    top, total, acc = state
    result = (acc / total).T.astype(BF16)
    log_sum = top * LOG2_SCALE + jnp.log2(total)
    high = log_sum.astype(BF16).astype(F32)
    middle = (log_sum - high).astype(BF16).astype(F32)
    low = log_sum - high - middle
    parts = jnp.concatenate([high, middle, low, jnp.zeros((13, count), F32)], axis=0)
    for n in range(count // SUB):
        out_ref[n, :SUB] = result[n * SUB : (n + 1) * SUB]
        moved = parts if n == 0 else pltpu.roll(parts, count - n * SUB, 1)
        out_ref[n, SUB:] = moved[:, :HD].astype(BF16)


def attend(name, spans, q, kvs, group, state=None, last=True):
    count = q.shape[0]
    if last:
        outs = [jax.ShapeDtypeStruct((count // SUB, PACKED, HD), BF16)]
    else:
        outs = [
            jax.ShapeDtypeStruct((1, count), F32),
            jax.ShapeDtypeStruct((1, count), F32),
            jax.ShapeDtypeStruct((HD, count), F32),
        ]
    kernel = functools.partial(attend_kernel, group, state is not None, last, len(kvs))
    state = () if state is None else tuple(state)
    specs = [SM] + [VM] * (1 + len(kvs) + len(state))
    return call(kernel, name, outs, specs)(spans, q, *kvs, *state)


def plane_order(h):
    g, j = h // 5, h % 5
    return 16 + g if j == 4 else 4 * j + g


def fresh_kernel(q_ref, kv_ref, out_ref, log_ref):
    width = q_ref.shape[1]
    lanes = lax.broadcasted_iota(jnp.int32, (SUB, HD), 1)
    logs = jnp.zeros((SUB, HD), F32)
    for h in range(width // HD):
        at = h * HD
        q = q_ref[:, at : at + HD]
        k = kv_ref[:, at : at + HD]
        v = kv_ref[:, width + at : width + at + HD]
        s = lax.dot_general(q, k, (((1,), (1,)), ((), ())), preferred_element_type=F32)
        top = jnp.max(s, axis=1, keepdims=True)
        w = jnp.exp2((s - top) * LOG2_SCALE)
        total = jnp.sum(w, axis=1, keepdims=True)
        out_ref[:, at : at + HD] = (
            jnp.dot(w.astype(BF16), v, preferred_element_type=F32) / total
        )
        logs = jnp.where(lanes == plane_order(h), top * LOG2_SCALE + jnp.log2(total), logs)
    log_ref[...] = logs


def merge_kernel(plane_ref, line_ref, fresh_ref, fresh_log_ref, out_ref):
    def logs_of(ref):
        rows = jnp.sum(ref[:, SUB:, :].astype(F32), axis=1)
        return rows.T[:SUB]

    plane_log, line_log = logs_of(plane_ref), logs_of(line_ref)
    fresh_log = fresh_log_ref[...]
    fresh_plane, fresh_line = fresh_log[:, :16], fresh_log[:, 16:20]
    line_a, line_b = line_log[:, :4], line_log[:, 4:]

    top = jnp.maximum(plane_log, fresh_plane)
    a, b = jnp.exp2(plane_log - top), jnp.exp2(fresh_plane - top)
    scale = 1.0 / (a + b)
    a, b = a * scale, b * scale
    top = jnp.maximum(jnp.maximum(line_a, line_b), fresh_line)
    la, lb, lf = (jnp.exp2(value - top) for value in (line_a, line_b, fresh_line))
    scale = 1.0 / (la + lb + lf)
    la, lb, lf = la * scale, lb * scale, lf * scale
    for h in range(20):
        at = h * HD
        fresh = fresh_ref[:, at : at + HD]
        n = plane_order(h)
        if n < 16:
            value = a[:, n : n + 1] * plane_ref[n, :SUB].astype(F32) + b[:, n : n + 1] * fresh
        else:
            g = n - 16
            value = (
                la[:, g : g + 1] * line_ref[g, :SUB].astype(F32)
                + lb[:, g : g + 1] * line_ref[4 + g, :SUB].astype(F32)
                + lf[:, g : g + 1] * fresh
            )
        out_ref[:, at : at + HD] = value.astype(BF16)


def round_pairs(r, planes):
    pairs = []
    for z in range(planes):
        for yl in range(2):
            for g in range(4):
                target = 4 * ((z % 4 + r) % 4) + g
                pairs.append(((z * 2 + yl) * 4 + g, (target * 2 + yl) * 4 + z // 4))
    return pairs


def step_pairs(dy):
    pairs = []
    for y in range(4):
        t = (y + dy) % 4
        pairs.append(((y % 2) * 2 + y // 2, (t % 2) * 2 + t // 2))
    return pairs


def per_device(fresh_q, fresh_k, fresh_v, stale_k, stale_v, scale_exps):
    z, yl, yh, c = (lax.axis_index(name) for name in ("z", "yl", "yh", "c"))
    shape = jax.ShapeDtypeStruct
    prepared = call(
        prepare_kernel,
        "prepare",
        [shape((PATCH, 2 * HD), BF16)] * 5
        + [
            shape((16, SUB, HD), BF16),
            shape((8, SUB, HD), BF16),
            shape((SUB, 2 * fresh_k.shape[1]), BF16),
        ],
        [SM] + [VM] * 6,
    )((z % 4).reshape(1), stale_k, stale_v, scale_exps, fresh_q, fresh_k, fresh_v)
    rounds, kv_line, q_plane, q_line, fresh_kv = prepared[:4], *prepared[4:]

    arrived = [
        lax.ppermute(rounds[r], ("z", "yl", "yh", "c"), round_pairs(r, 16)) for r in range(4)
    ]
    q_plane = lax.all_to_all(q_plane, "z", split_axis=0, concat_axis=0, tiled=True)
    q_plane = q_plane.reshape(16 * SUB, HD)
    q_line = lax.all_to_all(q_line, ("yl", "yh", "c"), split_axis=0, concat_axis=0, tiled=True)
    q_line = q_line.reshape(8 * SUB, HD)
    kv_line = lax.all_gather(kv_line, "z", axis=0, tiled=True)
    fresh_kv = lax.all_gather(fresh_kv, ("yh", "c"), axis=0, tiled=True)

    fresh, fresh_log = call(
        fresh_kernel,
        "own_patch",
        [shape(fresh_q.shape, F32), shape((SUB, HD), F32)],
        [VM] * 2,
    )(fresh_q, fresh_kv)

    own = jnp.arange(16, dtype=jnp.int32) == z
    low = jnp.where(own, PATCH * yl, -1)
    spans = jnp.stack([low, jnp.where(own, low + PATCH, -1)], axis=1)
    (line,) = attend("line_heads", spans, q_line, [kv_line], 8)
    line = lax.all_to_all(line, ("yl", "yh", "c"), split_axis=0, concat_axis=0, tiled=True)

    j = z // 4
    y = 2 * yh + yl
    state = None
    for chunk in CHUNKS:
        shard = jnp.concatenate([arrived[r] for r in chunk], axis=0)
        same = jnp.concatenate(
            [shard if dy == 0 else lax.ppermute(shard, ("yl", "yh"), step_pairs(dy)) for dy in STEPS_Y],
            axis=0,
        )
        other = lax.ppermute(same, "c", [(0, 1), (1, 0)])
        lows = []
        for core in (c, 1 - c):
            for dy in STEPS_Y:
                source = (y + 4 - dy) % 4
                for r in chunk:
                    patch = 4 * ((source // 2) * 2 + core) + (j + 4 - r) % 4
                    lows.append(SUB * patch if dy % 2 == 0 else jnp.int32(-SUB))
        low = jnp.stack([value.astype(jnp.int32) for value in lows])
        spans = jnp.stack([low, low + SUB], axis=1)
        last = chunk == CHUNKS[-1]
        state = attend(
            "plane_heads_last" if last else "plane_heads", spans, q_plane, [same, other], 8, state, last
        )
    (plane,) = state
    plane = lax.all_to_all(plane, "z", split_axis=0, concat_axis=0, tiled=True)

    (out,) = call(merge_kernel, "merge", [shape(fresh_q.shape, BF16)], [VM] * 4)(
        plane, line, fresh, fresh_log
    )
    return out


def solution(mesh):
    devices = np.asarray(mesh.devices).reshape(4, 16, 2, 2, 2)
    fine = Mesh(devices, ("x", "z", "yl", "yh", "c"))
    tokens = P(("x", "z", "yl", "yh", "c"), None)
    stored = P(("x", "z", "yl"), ("yh", "c"))
    in_specs = (tokens, tokens, tokens, stored, stored, P(("x", "z", "yl"), None))
    return jax.shard_map(
        per_device, mesh=fine, in_specs=in_specs, out_specs=tokens, check_vma=False
    )
```

time: 480 us -> 150 us (0.31)
  waiting for transfers between devices: 301 us -> 9.39 us
  starting transfers between devices: 19.1 us -> 95.6 us
  blocking collectives: 69.2 us -> 0 us
  local copies, waits for them, and re-layouts: 54 us -> 9.25 us
  Pallas kernels: 0 us -> 20.6 us
  matrix products: 12.9 us -> 0 us
  other arithmetic: 9.27 us -> 0.05 us
    all_gather x2, waiting for transfers between devices: 281 us -> 0.27 us  [the longest x1 0.27 us: per_device(): fresh_kv = lax.all_gather(fresh_kv, ('yh', 'c'), axis=0, tiled=True)]
    ppermute x0 -> x12, starting transfers between devices: none -> 60.3 us  [the longest x4 25.1 us: per_device(): lax.ppermute(rounds[r], ('z', 'yl', 'yh', 'c'), round_pairs(r, 16))]
    all_gather x1 -> x0, blocking collectives: 57.5 us -> none  [per_device(): all_exps = lax.all_gather(scale_exps, 'patch', axis=0, tiled=True)]
    dynamic_slice x24 -> x0, local copies, waits for them, and re-layouts: 46.7 us -> none  [attend(): finished, unused = lax.scan(one_block, running, items)]
    pallas_call x0 -> x6, Pallas kernels: none -> 20.6 us  [the longest x3 13.2 us: attend(): return call(kernel, name, outs, specs)(spans, q, *kvs, *state)]
    all_to_all x3 -> x4, starting transfers between devices: 19.1 us -> 35.3 us  [the longest x1 13.6 us: per_device(): lax.all_to_all(q_plane, 'z', split_axis=0, concat_axis=0, tiled=True)]
    dot_general x10 -> x0, matrix products: 12.9 us -> none  [the longest x5 7.44 us: one_block(): jnp.einsum('rhk,khd->rhd', expon.astype(jnp.bfloat16), value_full.reshape...]
    all_to_all x1 -> x0, blocking collectives: 11.6 us -> none  [per_device(): lax.all_to_all(result, 'head', split_axis=0, concat_axis=1, tiled=True)]
  transfers between devices with their start and end apart: 5 -> 18, of which waited for: 4 -> 2; matrix products, arithmetic and copies ran while one was open for 1% -> 1% of each run, Pallas kernels for 0% -> 12%
where the time goes in v1:
time: 150 us; the launch traced here: 149 us
  starting transfers between devices  95.6 us (64%)
  Pallas kernels  20.6 us (14%)
  between operations  14 us (9%)
  waiting for transfers between devices  9.39 us (6%)
  local copies, waits for them, and re-layouts  9.25 us (6%)
    ppermute x4, starting transfers between devices, per_device(): lax.ppermute(rounds[r], ('z', 'yl', 'yh', 'c'), round_pairs(r, 16))  25.1 us
    ppermute x6, starting transfers between devices, per_device(): lax.ppermute(shard, ('yl', 'yh'), step_pairs(dy))  21.4 us
    ppermute x2, starting transfers between devices, per_device(): other = lax.ppermute(same, 'c', [(0, 1), (1, 0)])  13.7 us
    all_to_all x1, starting transfers between devices, per_device(): lax.all_to_all(q_plane, 'z', split_axis=0, concat_axis=0, tiled=True)  13.6 us
    pallas_call x3, Pallas kernels, attend(): return call(kernel, name, outs, specs)(spans, q, *kvs, *state)  13.2 us
    all_to_all x1, starting transfers between devices, per_device(): lax.all_to_all(line, ('yl', 'yh', 'c'), split_axis=0, concat_axis=0, tile...  9.2 us
    all_to_all x1, starting transfers between devices, per_device(): plane = lax.all_to_all(plane, 'z', split_axis=0, concat_axis=0, tiled=True)  9.06 us
    all_to_all x1, waiting for transfers between devices, per_device(): plane = lax.all_to_all(plane, 'z', split_axis=0, concat_axis=0, tiled=True)  9.05 us
  transfers between devices with their start and end apart: 18, of which 2 were waited for; matrix products, arithmetic and copies ran while one was open for 1% of the time, Pallas kernels for 12%

profile of v1, /device:TPU:1, one launch (start us, length us, event | category | flops | bytes accessed | tf_op | source)
XLA Modules:
  0.0 149.0 jit_solution(15626821353566202540)
XLA Ops:
  6.5 0.8 copy.10.exps_ref
  7.4 0.9 copy-done.2
  8.3 0.9 copy-done.4
  9.2 0.9 copy-done.5
  10.2 0.9 copy-done.6
  11.1 0.9 copy-done.7
  12.1 1.0 prepare.1
  13.1 4.9 %collective-permute-start.6 = (bf16[192,256]{1,0:T(8,128)(2,1)S(1)}, bf16[192,256]{1,0:T(8,128)(2,1)S(1)}, u32[]{:S(2)}, u32[]{:S(2)}) collective-permute-start(bf16[192,256]{1,0:T(8,128)(2,1)S(1)} %get-tuple-element.21), channel_id=1, source_target_pairs={{0,0},{1,8},{2,16},{3,24},{4,4},{5,12},{6,20},{7,28},{8,32},{9,40}... | collective-permute-start | bytes 294920 | tf_op jit(solution)/shard_map/ppermute | solution.py:250
  18.0 8.5 %collective-permute-start.7 = (bf16[192,256]{1,0:T(8,128)(2,1)S(1)}, bf16[192,256]{1,0:T(8,128)(2,1)S(1)}, u32[]{:S(2)}, u32[]{:S(2)}) collective-permute-start(bf16[192,256]{1,0:T(8,128)(2,1)S(1)} %get-tuple-element.22), channel_id=1, source_target_pairs={{0,32},{1,40},{2,48},{3,56},{4,36},{5,44},{6,52},{7,60},{8,64},{9,... | collective-permute-start | bytes 294920 | tf_op jit(solution)/shard_map/ppermute | solution.py:250
  26.6 13.6 %all-to-all-start = ((bf16[16,48,128]{2,1,0:T(8,128)(2,1)}), bf16[16,48,128]{2,1,0:T(8,128)(2,1)S(1)}, u32[]{:S(2)}, u32[]{:S(2)}) async-start(bf16[16,48,128]{2,1,0:T(8,128)(2,1)} %get-tuple-element.18), calls=%async_computation | async-start | bytes 393216 | tf_op jit(solution)/shard_map/all_to_all | solution.py:252
  40.3 7.9 %collective-permute-start = (bf16[192,256]{1,0:T(8,128)(2,1)S(1)}, bf16[192,256]{1,0:T(8,128)(2,1)S(1)}, u32[]{:S(2)}, u32[]{:S(2)}) collective-permute-start(bf16[192,256]{1,0:T(8,128)(2,1)S(1)} %get-tuple-element.19), channel_id=1, source_target_pairs={{0,64},{1,72},{2,80},{3,88},{4,68},{5,76},{6,84},{7,92},{8,96},{9,... | collective-permute-start | bytes 294920 | tf_op jit(solution)/shard_map/ppermute | solution.py:250
  48.2 3.8 %collective-permute-start.1 = (bf16[192,256]{1,0:T(8,128)(2,1)S(1)}, bf16[192,256]{1,0:T(8,128)(2,1)S(1)}, u32[]{:S(2)}, u32[]{:S(2)}) collective-permute-start(bf16[192,256]{1,0:T(8,128)(2,1)S(1)} %get-tuple-element.20), channel_id=1, source_target_pairs={{0,96},{1,104},{2,112},{3,120},{4,100},{5,108},{6,116},{7,124},{8,... | collective-permute-start | bytes 294920 | tf_op jit(solution)/shard_map/ppermute | solution.py:250
  52.1 3.2 %collective-permute-start.8 = (bf16[384,256]{1,0:T(8,128)(2,1)S(1)}, bf16[384,256]{1,0:T(8,128)(2,1)S(1)}, u32[]{:S(2)}, u32[]{:S(2)}) collective-permute-start(bf16[384,256]{1,0:T(8,128)(2,1)S(1)} %get-tuple-element.31), channel_id=1, source_target_pairs={{0,4},{4,2},{2,6},{6,0},{1,5},{5,3},{3,7},{7,1},{8,12},{12,10},{10... | collective-permute-start | bytes 589832 | tf_op jit(solution)/shard_map/ppermute | solution.py:278
  55.3 6.1 %collective-permute-start.9 = (bf16[384,256]{1,0:T(8,128)(2,1)S(1)}, bf16[384,256]{1,0:T(8,128)(2,1)S(1)}, u32[]{:S(2)}, u32[]{:S(2)}) collective-permute-start(bf16[384,256]{1,0:T(8,128)(2,1)S(1)} %get-tuple-element.31), channel_id=1, source_target_pairs={{0,6},{4,0},{2,4},{6,2},{1,7},{5,1},{3,5},{7,3},{8,14},{12,8},{10,... | collective-permute-start | bytes 589832 | tf_op jit(solution)/shard_map/ppermute | solution.py:278
  61.4 3.1 %collective-permute-start.10 = (bf16[384,256]{1,0:T(8,128)(2,1)S(1)}, bf16[384,256]{1,0:T(8,128)(2,1)S(1)}, u32[]{:S(2)}, u32[]{:S(2)}) collective-permute-start(bf16[384,256]{1,0:T(8,128)(2,1)S(1)} %get-tuple-element.31), channel_id=1, source_target_pairs={{0,2},{4,6},{2,0},{6,4},{1,3},{5,7},{3,1},{7,5},{8,10},{12,14},{10... | collective-permute-start | bytes 589832 | tf_op jit(solution)/shard_map/ppermute | solution.py:278
  64.6 2.8 %collective-permute-start.2 = (bf16[384,256]{1,0:T(8,128)(2,1)S(1)}, bf16[384,256]{1,0:T(8,128)(2,1)S(1)}, u32[]{:S(2)}, u32[]{:S(2)}) collective-permute-start(bf16[384,256]{1,0:T(8,128)(2,1)S(1)} %get-tuple-element.35), channel_id=1, source_target_pairs={{0,4},{4,2},{2,6},{6,0},{1,5},{5,3},{3,7},{7,1},{8,12},{12,10},{10... | collective-permute-start | bytes 589832 | tf_op jit(solution)/shard_map/ppermute | solution.py:278
  67.3 3.7 %collective-permute-start.3 = (bf16[384,256]{1,0:T(8,128)(2,1)S(1)}, bf16[384,256]{1,0:T(8,128)(2,1)S(1)}, u32[]{:S(2)}, u32[]{:S(2)}) collective-permute-start(bf16[384,256]{1,0:T(8,128)(2,1)S(1)} %get-tuple-element.35), channel_id=1, source_target_pairs={{0,6},{4,0},{2,4},{6,2},{1,7},{5,1},{3,5},{7,3},{8,14},{12,8},{10,... | collective-permute-start | bytes 589832 | tf_op jit(solution)/shard_map/ppermute | solution.py:278
  71.1 2.5 %collective-permute-start.4 = (bf16[384,256]{1,0:T(8,128)(2,1)S(1)}, bf16[384,256]{1,0:T(8,128)(2,1)S(1)}, u32[]{:S(2)}, u32[]{:S(2)}) collective-permute-start(bf16[384,256]{1,0:T(8,128)(2,1)S(1)} %get-tuple-element.35), channel_id=1, source_target_pairs={{0,2},{4,6},{2,0},{6,4},{1,3},{5,7},{3,1},{7,5},{8,10},{12,14},{10... | collective-permute-start | bytes 589832 | tf_op jit(solution)/shard_map/ppermute | solution.py:278
  73.7 8.2 %collective-permute-start.11 = (bf16[1536,256]{1,0:T(8,128)(2,1)S(1)}, bf16[1536,256]{1,0:T(8,128)(2,1)S(1)}, u32[]{:S(2)}, u32[]{:S(2)}) collective-permute-start(bf16[1536,256]{1,0:T(8,128)(2,1)S(1)} %constant_dynamic-update-slice_fusion.9.refs_2_), channel_id=1, source_target_pairs={{0,1},{1,0},{2,3},{3,2},{4,5},{5,4},{6,7},{7,6},{8,9},{9,8},{10,11... | collective-permute-start | bytes 2359304 | tf_op jit(solution)/shard_map/ppermute | solution.py:281
  82.0 5.5 %collective-permute-start.5 = (bf16[1536,256]{1,0:T(8,128)(2,1)S(1)}, bf16[1536,256]{1,0:T(8,128)(2,1)S(1)}, u32[]{:S(2)}, u32[]{:S(2)}) collective-permute-start(bf16[1536,256]{1,0:T(8,128)(2,1)S(1)} %constant_dynamic-update-slice_fusion.2.refs_2_), channel_id=1, source_target_pairs={{0,1},{1,0},{2,3},{3,2},{4,5},{5,4},{6,7},{7,6},{8,9},{9,8},{10,11... | collective-permute-start | bytes 2359304 | tf_op jit(solution)/shard_map/ppermute | solution.py:281
  88.2 3.4 %all-to-all-start.2 = ((bf16[8,48,128]{2,1,0:T(8,128)(2,1)}), bf16[8,48,128]{2,1,0:T(8,128)(2,1)S(1)}, u32[]{:S(2)}, u32[]{:S(2)}) async-start(bf16[8,48,128]{2,1,0:T(8,128)(2,1)} %get-tuple-element.26), calls=%async_computation.2 | async-start | bytes 196608 | tf_op jit(solution)/shard_map/all_to_all | solution.py:254
  91.7 3.6 %plane_heads.1 = (f32[1,768]{1,0:T(1,128)S(1)}, f32[1,768]{1,0:T(1,128)S(1)}, f32[128,768]{1,0:T(8,128)S(1)}) custom-call(s32[16,2]{1,0:T(8,128)S(1)} %copy.11.refs_0_, bf16[768,128]{1,0:T(8,128)(2,1)S(1)} %bitcast.37, bf16[1536,256]{1,0:T(8,128)(2,1)S(1)} %constant_dynamic-update-slice_fusion.9.refs_2_, bf16[1536,256]{1,0:T(8,128)(2,1)S(1)} %collective-permute-done.11.refs_3_), custom_call_target="tpu_custom_call" | custom-call | tf_op jit(solution)/shard_map/plane_heads/pallas_call | solution.py:153
  95.4 5.7 %plane_heads_last.1 = bf16[16,64,128]{2,1,0:T(8,128)(2,1)} custom-call(s32[16,2]{1,0:T(8,128)S(1)} %copy.12.refs_0_, bf16[768,128]{1,0:T(8,128)(2,1)S(1)} %bitcast.38, bf16[1536,256]{1,0:T(8,128)(2,1)S(1)} %constant_dynamic-update-slice_fusion.2.refs_2_, bf16[1536,256]{1,0:T(8,128)(2,1)S(1)} %collective-permute-done.5.refs_3_, ...), custom_call_target="tpu_custom_call" | custom-call | tf_op jit(solution)/shard_map/plane_heads_last/pallas_call | solution.py:153
  101.1 9.1 %all-to-all-start.1 = ((bf16[16,64,128]{2,1,0:T(8,128)(2,1)}), bf16[16,64,128]{2,1,0:T(8,128)(2,1)S(1)}, u32[]{:S(2)}, u32[]{:S(2)}) async-start(bf16[16,64,128]{2,1,0:T(8,128)(2,1)} %plane_heads_last.1), calls=%async_computation.1 | async-start | bytes 524288 | tf_op jit(solution)/shard_map/all_to_all | solution.py:296
  110.3 1.4 copy-done.1
  111.7 3.8 %line_heads.1 = bf16[8,64,128]{2,1,0:T(8,128)(2,1)} custom-call(s32[16,2]{1,0:T(8,128)S(1)} %copy.13.refs_0_, bf16[384,128]{1,0:T(8,128)(2,1)S(1)} %bitcast.39, bf16[3072,256]{1,0:T(8,128)(2,1)S(1)} %copy-done.1), custom_call_target="tpu_custom_call" | custom-call | tf_op jit(solution)/shard_map/line_heads/pallas_call | solution.py:153
  115.6 9.0 %all-to-all-done.1.plane_ref = bf16[16,64,128]{2,1,0:T(8,128)(2,1)S(1)} async-done(((bf16[16,64,128]{2,1,0:T(8,128)(2,1)}), bf16[16,64,128]{2,1,0:T(8,128)(2,1)S(1)}, u32[]{:S(2)}, u32[]{:S(2)}) %all-to-all-start.1) | async-done | bytes 262176 | tf_op jit(solution)/shard_map/all_to_all | solution.py:296
  124.6 9.2 %all-to-all-start.3 = ((bf16[8,64,128]{2,1,0:T(8,128)(2,1)}), bf16[8,64,128]{2,1,0:T(8,128)(2,1)S(1)}, u32[]{:S(2)}, u32[]{:S(2)}) async-start(bf16[8,64,128]{2,1,0:T(8,128)(2,1)} %line_heads.1), calls=%async_computation.3 | async-start | bytes 262144 | tf_op jit(solution)/shard_map/all_to_all | solution.py:270
  133.8 0.3 all-gather.5.cloned.1.call-done.kv_ref
  134.1 1.5 %copy-done = bf16[192,5120]{1,0:T(8,128)(2,1)S(1)} copy-done((bf16[192,5120]{1,0:T(8,128)(2,1)S(1)}, bf16[192,5120]{1,0:T(8,128)(2,1)}, u32[]{:S(2)}) %copy-start) | copy-done | bytes 1966104
  135.6 5.2 %own_patch.1 = (f32[48,2560]{1,0:T(8,128)S(1)}, f32[48,128]{1,0:T(8,128)S(1)}) custom-call(bf16[48,2560]{1,0:T(8,128)(2,1)S(1)} %copy-done.3, bf16[192,5120]{1,0:T(8,128)(2,1)S(1)} %copy-done), custom_call_target="tpu_custom_call" | custom-call | tf_op jit(solution)/shard_map/own_patch/pallas_call | solution.py:259
  140.8 1.3 merge.1
  (54 shorter events, 1.0 us)
Async XLA Ops:
  6.5 103.8 %all-gather.3.cloned.1.call-start = ((), (), s32[]{:S(2)}) async-start(), calls=%async_computation.4 | async-start | bytes 1671168 | tf_op jit(solution)/shard_map/all_gather | solution.py:256
  7.3 0.9 copy-start.2
  8.3 0.9 copy-start.4
  9.2 0.9 copy-start.5
  10.2 0.9 copy-start.6
  11.1 0.9 copy-start.7
  13.1 38.9 %collective-permute-start.6 = (bf16[192,256]{1,0:T(8,128)(2,1)S(1)}, bf16[192,256]{1,0:T(8,128)(2,1)S(1)}, u32[]{:S(2)}, u32[]{:S(2)}) collective-permute-start(bf16[192,256]{1,0:T(8,128)(2,1)S(1)} %get-tuple-element.21), channel_id=1, source_target_pairs={{0,0},{1,8},{2,16},{3,24},{4,4},{5,12},{6,20},{7,28},{8,32},{9,40}... | collective-permute-start | bytes 294920 | tf_op jit(solution)/shard_map/ppermute | solution.py:250
  18.0 34.0 %collective-permute-start.7 = (bf16[192,256]{1,0:T(8,128)(2,1)S(1)}, bf16[192,256]{1,0:T(8,128)(2,1)S(1)}, u32[]{:S(2)}, u32[]{:S(2)}) collective-permute-start(bf16[192,256]{1,0:T(8,128)(2,1)S(1)} %get-tuple-element.22), channel_id=1, source_target_pairs={{0,32},{1,40},{2,48},{3,56},{4,36},{5,44},{6,52},{7,60},{8,64},{9,... | collective-permute-start | bytes 294920 | tf_op jit(solution)/shard_map/ppermute | solution.py:250
  26.6 61.6 %all-to-all-start = ((bf16[16,48,128]{2,1,0:T(8,128)(2,1)}), bf16[16,48,128]{2,1,0:T(8,128)(2,1)S(1)}, u32[]{:S(2)}, u32[]{:S(2)}) async-start(bf16[16,48,128]{2,1,0:T(8,128)(2,1)} %get-tuple-element.18), calls=%async_computation | async-start | bytes 393216 | tf_op jit(solution)/shard_map/all_to_all | solution.py:252
  40.2 93.8 %all-gather.5.cloned.1.call-start = ((), (), s32[]{:S(2)}) async-start(), calls=%async_computation.5 | async-start | bytes 2457600 | tf_op jit(solution)/shard_map/all_gather | solution.py:257
  40.3 24.2 %collective-permute-start = (bf16[192,256]{1,0:T(8,128)(2,1)S(1)}, bf16[192,256]{1,0:T(8,128)(2,1)S(1)}, u32[]{:S(2)}, u32[]{:S(2)}) collective-permute-start(bf16[192,256]{1,0:T(8,128)(2,1)S(1)} %get-tuple-element.19), channel_id=1, source_target_pairs={{0,64},{1,72},{2,80},{3,88},{4,68},{5,76},{6,84},{7,92},{8,96},{9,... | collective-permute-start | bytes 294920 | tf_op jit(solution)/shard_map/ppermute | solution.py:250
  48.2 16.4 %collective-permute-start.1 = (bf16[192,256]{1,0:T(8,128)(2,1)S(1)}, bf16[192,256]{1,0:T(8,128)(2,1)S(1)}, u32[]{:S(2)}, u32[]{:S(2)}) collective-permute-start(bf16[192,256]{1,0:T(8,128)(2,1)S(1)} %get-tuple-element.20), channel_id=1, source_target_pairs={{0,96},{1,104},{2,112},{3,120},{4,100},{5,108},{6,116},{7,124},{8,... | collective-permute-start | bytes 294920 | tf_op jit(solution)/shard_map/ppermute | solution.py:250
  52.1 19.0 %collective-permute-start.8 = (bf16[384,256]{1,0:T(8,128)(2,1)S(1)}, bf16[384,256]{1,0:T(8,128)(2,1)S(1)}, u32[]{:S(2)}, u32[]{:S(2)}) collective-permute-start(bf16[384,256]{1,0:T(8,128)(2,1)S(1)} %get-tuple-element.31), channel_id=1, source_target_pairs={{0,4},{4,2},{2,6},{6,0},{1,5},{5,3},{3,7},{7,1},{8,12},{12,10},{10... | collective-permute-start | bytes 589832 | tf_op jit(solution)/shard_map/ppermute | solution.py:278
  55.3 18.3 %collective-permute-start.9 = (bf16[384,256]{1,0:T(8,128)(2,1)S(1)}, bf16[384,256]{1,0:T(8,128)(2,1)S(1)}, u32[]{:S(2)}, u32[]{:S(2)}) collective-permute-start(bf16[384,256]{1,0:T(8,128)(2,1)S(1)} %get-tuple-element.31), channel_id=1, source_target_pairs={{0,6},{4,0},{2,4},{6,2},{1,7},{5,1},{3,5},{7,3},{8,14},{12,8},{10,... | collective-permute-start | bytes 589832 | tf_op jit(solution)/shard_map/ppermute | solution.py:278
  61.4 12.2 %collective-permute-start.10 = (bf16[384,256]{1,0:T(8,128)(2,1)S(1)}, bf16[384,256]{1,0:T(8,128)(2,1)S(1)}, u32[]{:S(2)}, u32[]{:S(2)}) collective-permute-start(bf16[384,256]{1,0:T(8,128)(2,1)S(1)} %get-tuple-element.31), channel_id=1, source_target_pairs={{0,2},{4,6},{2,0},{6,4},{1,3},{5,7},{3,1},{7,5},{8,10},{12,14},{10... | collective-permute-start | bytes 589832 | tf_op jit(solution)/shard_map/ppermute | solution.py:278
  64.6 17.4 %collective-permute-start.2 = (bf16[384,256]{1,0:T(8,128)(2,1)S(1)}, bf16[384,256]{1,0:T(8,128)(2,1)S(1)}, u32[]{:S(2)}, u32[]{:S(2)}) collective-permute-start(bf16[384,256]{1,0:T(8,128)(2,1)S(1)} %get-tuple-element.35), channel_id=1, source_target_pairs={{0,4},{4,2},{2,6},{6,0},{1,5},{5,3},{3,7},{7,1},{8,12},{12,10},{10... | collective-permute-start | bytes 589832 | tf_op jit(solution)/shard_map/ppermute | solution.py:278
  67.3 14.6 %collective-permute-start.3 = (bf16[384,256]{1,0:T(8,128)(2,1)S(1)}, bf16[384,256]{1,0:T(8,128)(2,1)S(1)}, u32[]{:S(2)}, u32[]{:S(2)}) collective-permute-start(bf16[384,256]{1,0:T(8,128)(2,1)S(1)} %get-tuple-element.35), channel_id=1, source_target_pairs={{0,6},{4,0},{2,4},{6,2},{1,7},{5,1},{3,5},{7,3},{8,14},{12,8},{10,... | collective-permute-start | bytes 589832 | tf_op jit(solution)/shard_map/ppermute | solution.py:278
  71.1 10.9 %collective-permute-start.4 = (bf16[384,256]{1,0:T(8,128)(2,1)S(1)}, bf16[384,256]{1,0:T(8,128)(2,1)S(1)}, u32[]{:S(2)}, u32[]{:S(2)}) collective-permute-start(bf16[384,256]{1,0:T(8,128)(2,1)S(1)} %get-tuple-element.35), channel_id=1, source_target_pairs={{0,2},{4,6},{2,0},{6,4},{1,3},{5,7},{3,1},{7,5},{8,10},{12,14},{10... | collective-permute-start | bytes 589832 | tf_op jit(solution)/shard_map/ppermute | solution.py:278
  73.7 18.1 %collective-permute-start.11 = (bf16[1536,256]{1,0:T(8,128)(2,1)S(1)}, bf16[1536,256]{1,0:T(8,128)(2,1)S(1)}, u32[]{:S(2)}, u32[]{:S(2)}) collective-permute-start(bf16[1536,256]{1,0:T(8,128)(2,1)S(1)} %constant_dynamic-update-slice_fusion.9.refs_2_), channel_id=1, source_target_pairs={{0,1},{1,0},{2,3},{3,2},{4,5},{5,4},{6,7},{7,6},{8,9},{9,8},{10,11... | collective-permute-start | bytes 2359304 | tf_op jit(solution)/shard_map/ppermute | solution.py:281
  82.0 13.4 %collective-permute-start.5 = (bf16[1536,256]{1,0:T(8,128)(2,1)S(1)}, bf16[1536,256]{1,0:T(8,128)(2,1)S(1)}, u32[]{:S(2)}, u32[]{:S(2)}) collective-permute-start(bf16[1536,256]{1,0:T(8,128)(2,1)S(1)} %constant_dynamic-update-slice_fusion.2.refs_2_), channel_id=1, source_target_pairs={{0,1},{1,0},{2,3},{3,2},{4,5},{5,4},{6,7},{7,6},{8,9},{9,8},{10,11... | collective-permute-start | bytes 2359304 | tf_op jit(solution)/shard_map/ppermute | solution.py:281
  88.2 12.9 %all-to-all-start.2 = ((bf16[8,48,128]{2,1,0:T(8,128)(2,1)}), bf16[8,48,128]{2,1,0:T(8,128)(2,1)S(1)}, u32[]{:S(2)}, u32[]{:S(2)}) async-start(bf16[8,48,128]{2,1,0:T(8,128)(2,1)} %get-tuple-element.26), calls=%async_computation.2 | async-start | bytes 196608 | tf_op jit(solution)/shard_map/all_to_all | solution.py:254
  95.4 38.7 %copy-start.3 = (bf16[48,2560]{1,0:T(8,128)(2,1)S(1)}, bf16[48,2560]{1,0:T(8,128)(2,1)}, u32[]{:S(2)}) copy-start(bf16[48,2560]{1,0:T(8,128)(2,1)} %q_ref.3) | copy-start | bytes 737284
  101.1 23.5 %all-to-all-start.1 = ((bf16[16,64,128]{2,1,0:T(8,128)(2,1)}), bf16[16,64,128]{2,1,0:T(8,128)(2,1)S(1)}, u32[]{:S(2)}, u32[]{:S(2)}) async-start(bf16[16,64,128]{2,1,0:T(8,128)(2,1)} %plane_heads_last.1), calls=%async_computation.1 | async-start | bytes 524288 | tf_op jit(solution)/shard_map/all_to_all | solution.py:296
  110.3 1.4 copy-start.1
  124.6 16.2 %all-to-all-start.3 = ((bf16[8,64,128]{2,1,0:T(8,128)(2,1)}), bf16[8,64,128]{2,1,0:T(8,128)(2,1)S(1)}, u32[]{:S(2)}, u32[]{:S(2)}) async-start(bf16[8,64,128]{2,1,0:T(8,128)(2,1)} %line_heads.1), calls=%async_computation.3 | async-start | bytes 262144 | tf_op jit(solution)/shard_map/all_to_all | solution.py:270
  134.1 1.5 %copy-start = (bf16[192,5120]{1,0:T(8,128)(2,1)S(1)}, bf16[192,5120]{1,0:T(8,128)(2,1)}, u32[]{:S(2)}) copy-start(bf16[192,5120]{1,0:T(8,128)(2,1)} %all-gather.5.cloned.1.call-done.kv_ref) | copy-start | bytes 5898244
Sparse Core Ops, SparseCore 0:
  13.2 80.9 all-gather.2
  96.3 37.7 all-gather.4

commit v2 on v0

v2 whole, which is shorter than its diff:
```python
import functools
import math

import jax
import jax.numpy as jnp
import numpy as np
from jax import lax
from jax.experimental import pallas as pl
from jax.experimental.pallas import tpu as pltpu
from jax.sharding import Mesh, PartitionSpec as P


HD = 128
LOG2_SCALE = math.log2(math.e) / math.sqrt(HD)
LOWEST = -1e30
SUB = 48
PATCH = 192
PACKED = 112
VMEM_BYTES = 24 * 2**20
VM = pl.BlockSpec(memory_space=pltpu.VMEM)
SM = pl.BlockSpec(memory_space=pltpu.SMEM)
BF16, F32 = jnp.bfloat16, jnp.float32


def call(kernel, name, outs, in_specs):
    return pl.pallas_call(
        kernel,
        out_shape=outs,
        in_specs=in_specs,
        out_specs=[VM] * len(outs),
        compiler_params=pltpu.CompilerParams(vmem_limit_bytes=VMEM_BYTES),
        name=name,
    )


def stored_kernel(first_ref, k_ref, v_ref, exps_ref, *rounds):
    scales = jnp.exp2(exps_ref[...].astype(F32))
    scales = jnp.concatenate([scales, jnp.zeros((6, PATCH), F32)], axis=0).T
    k_scale, v_scale = scales[:, 0:1], scales[:, 1:2]

    def put(ref, row, column):
        k = k_ref[:, pl.ds(column, HD)].astype(F32) * k_scale
        v = v_ref[:, pl.ds(column, HD)].astype(F32) * v_scale
        ref[row : row + PATCH, :HD] = k.astype(BF16)
        ref[row : row + PATCH, HD:] = v.astype(BF16)

    for r in range(4):
        j = (first_ref[0] + r * first_ref[1]) % 4
        put(rounds[r], 0, pl.multiple_of(j * HD, HD))
    put(rounds[0], PATCH, 4 * HD)


def fresh_layout_kernel(q_ref, fk_ref, fv_ref, q_out_ref, fresh_ref):
    for g in range(4):
        for j in range(4):
            at = (5 * g + j) * HD
            q_out_ref[4 * j + g, :SUB] = q_ref[:, at : at + HD]
            at = (5 * g + 4) * HD
            q_out_ref[4 * j + g, SUB:] = q_ref[:, at : at + HD]
    width = fk_ref.shape[1]
    fresh_ref[:, :width] = fk_ref[...]
    fresh_ref[:, width:] = fv_ref[...]


def start_state(count):
    return (
        jnp.full((1, count), LOWEST, F32),
        jnp.zeros((1, count), F32),
        jnp.zeros((HD, count), F32),
    )


def accumulate(state, queries, kv_refs, spans_ref, groups):
    top, total, acc = state
    lanes = lax.broadcasted_iota(jnp.int32, (1, queries.shape[0]), 1)
    for group in groups:
        k = jnp.concatenate([kv_refs[n][row : row + PATCH, :HD] for n, row, _ in group], axis=0)
        v = jnp.concatenate([kv_refs[n][row : row + PATCH, HD:] for n, row, _ in group], axis=0)
        s = lax.dot_general(k, queries, (((1,), (1,)), ((), ())), preferred_element_type=F32)
        blocks, masks = [], []
        new_top = top
        for n, (_, _, span) in enumerate(group):
            block = s[n * PATCH : (n + 1) * PATCH]
            low = spans_ref[span]
            mask = (lanes >= low) & (lanes < low + SUB)
            block_top = jnp.max(block, axis=0, keepdims=True)
            new_top = jnp.maximum(new_top, jnp.where(mask, LOWEST, block_top))
            blocks.append(block)
            masks.append(mask)
        shift = new_top * LOG2_SCALE
        weights = []
        shrink = jnp.exp2(top * LOG2_SCALE - shift)
        total = total * shrink
        for block, mask in zip(blocks, masks):
            w = jnp.exp2(block * LOG2_SCALE - jnp.where(mask, -LOWEST, shift))
            total = total + jnp.sum(w, axis=0, keepdims=True)
            weights.append(w.astype(BF16))
        w = jnp.concatenate(weights, axis=0)
        acc = acc * shrink + lax.dot_general(
            v, w, (((0,), (0,)), ((), ())), preferred_element_type=F32
        )
        top = new_top
    return top, total, acc


def finish(state):
    top, total, acc = state
    log_sum = top * LOG2_SCALE + jnp.log2(total)
    high = log_sum.astype(BF16).astype(F32)
    middle = (log_sum - high).astype(BF16).astype(F32)
    return (acc / total).T.astype(BF16), [high, middle, log_sum - high - middle]


def queries_of(q_ref):
    count = q_ref.shape[0] * SUB
    return q_ref[:, :SUB].reshape(count, HD), q_ref[:, SUB:].reshape(count, HD)


def attend_kernel(groups, n_kv, has_state, last, spans_ref, q_ref, *refs):
    kv_refs, refs = refs[:n_kv], refs[n_kv:]
    results, rows = [], []
    for n, queries in enumerate(queries_of(q_ref)):
        if has_state:
            state = tuple(ref[...] for ref in refs[3 * n : 3 * n + 3])
        else:
            state = start_state(queries.shape[0])
        state = accumulate(state, queries, kv_refs, spans_ref, groups[n])
        if last:
            result, log_rows = finish(state)
            results.append(result)
            rows += log_rows
        else:
            for ref, value in zip(refs[6 * has_state + 3 * n :], state):
                ref[...] = value
    if not last:
        return
    out_ref = refs[-1]
    count = results[0].shape[0]
    rows = jnp.concatenate(rows + [jnp.zeros((10, count), F32)], axis=0)
    for n in range(count // SUB):
        out_ref[n, :SUB] = results[0][n * SUB : (n + 1) * SUB]
        out_ref[n, SUB : 2 * SUB] = results[1][n * SUB : (n + 1) * SUB]
        moved = rows if n == 0 else pltpu.roll(rows, count - n * SUB, 1)
        out_ref[n, 2 * SUB :] = moved[:, :HD].astype(BF16)


def attend(name, spans, q, shards, state=None, last=False):
    arrays = []
    for array, _, _ in shards:
        if not any(array is other for other in arrays):
            arrays.append(array)
    main, extra = [], []
    for array, row, span in shards:
        at = [n for n, other in enumerate(arrays) if other is array][0]
        main += [(at, row + (r + 1 if r else 0) * PATCH, span + r) for r in range(4)]
        extra.append((at, row + PATCH, span))
    groups = ([main[n : n + 8] for n in range(0, len(main), 8)], [extra])
    count = q.shape[0] * SUB
    shape = jax.ShapeDtypeStruct
    outs = [shape((1, count), F32), shape((1, count), F32), shape((HD, count), F32)] * 2
    if last:
        outs = [shape((q.shape[0], PACKED, HD), BF16)]
    state = () if state is None else tuple(state)
    kernel = functools.partial(attend_kernel, groups, len(arrays), bool(state), last)
    specs = [SM] + [VM] * (1 + len(arrays) + len(state))
    return call(kernel, name, outs, specs)(spans, q, *arrays, *state)


def plane_order(h):
    g, j = h // 5, h % 5
    return 16 + g if j == 4 else 4 * j + g


def fresh_kernel(q_ref, near_ref, far_ref, out_ref, log_ref):
    kv_refs = (near_ref, far_ref)
    width = q_ref.shape[1]
    lanes = lax.broadcasted_iota(jnp.int32, (SUB, HD), 1)
    logs = jnp.zeros((SUB, HD), F32)
    for h in range(width // HD):
        at = h * HD
        q = q_ref[:, at : at + HD]
        k = jnp.concatenate([ref[:, at : at + HD] for ref in kv_refs], axis=0)
        v = jnp.concatenate([ref[:, width + at : width + at + HD] for ref in kv_refs], axis=0)
        s = lax.dot_general(q, k, (((1,), (1,)), ((), ())), preferred_element_type=F32)
        top = jnp.max(s, axis=1, keepdims=True)
        w = jnp.exp2((s - top) * LOG2_SCALE)
        total = jnp.sum(w, axis=1, keepdims=True)
        out_ref[:, at : at + HD] = (
            jnp.dot(w.astype(BF16), v, preferred_element_type=F32) / total
        )
        logs = jnp.where(lanes == plane_order(h), top * LOG2_SCALE + jnp.log2(total), logs)
    log_ref[...] = logs


def merge_kernel(both_ref, fresh_ref, fresh_log_ref, out_ref):
    main_ref, extra_ref = both_ref.at[:, :SUB], both_ref.at[:, SUB : 2 * SUB]
    rows = both_ref[:, 2 * SUB :].astype(F32)
    main_log = jnp.sum(rows[:, 0:3], axis=1).T[:SUB]
    extra_log = jnp.sum(rows[:, 3:6], axis=1).T[:SUB]
    fresh_log = fresh_log_ref[...]
    fresh_main, fresh_extra = fresh_log[:, :16], fresh_log[:, 16:20]

    top = jnp.maximum(main_log, fresh_main)
    a, b = jnp.exp2(main_log - top), jnp.exp2(fresh_main - top)
    scale = 1.0 / (a + b)
    a, b = a * scale, b * scale
    parts = [extra_log[:, 4 * j : 4 * j + 4] for j in range(4)] + [fresh_extra]
    top = functools.reduce(jnp.maximum, parts)
    parts = [jnp.exp2(part - top) for part in parts]
    scale = 1.0 / functools.reduce(jnp.add, parts)
    parts = [part * scale for part in parts]
    for h in range(20):
        at = h * HD
        fresh = fresh_ref[:, at : at + HD]
        n = plane_order(h)
        if n < 16:
            value = a[:, n : n + 1] * main_ref[n].astype(F32) + b[:, n : n + 1] * fresh
        else:
            g = n - 16
            value = parts[4][:, g : g + 1] * fresh
            for j in range(4):
                value += parts[j][:, g : g + 1] * extra_ref[4 * j + g].astype(F32)
        out_ref[:, at : at + HD] = value.astype(BF16)


def round_pairs(r):
    pairs = []
    for z in range(16):
        for yl in range(2):
            for yh in range(2):
                for c in range(2):
                    g, move = yh * 2 + c, (z // 2 % 2) ^ c
                    plane = 4 * ((z // 4 + (r if c == 0 else 4 - r)) % 4) + g
                    target = ((plane * 2 + (yl ^ move)) * 2 + (yh ^ move)) * 2 + z % 2
                    pairs.append(((z * 2 + yl) * 4 + g, target))
    return pairs


def per_device(fresh_q, fresh_k, fresh_v, stale_k, stale_v, scale_exps):
    z, yl, yh, c = (lax.axis_index(name) for name in ("z", "yl", "yh", "c"))
    shape = jax.ShapeDtypeStruct
    j = z // 4

    rounds = call(
        stored_kernel,
        "stored_scaled",
        [shape((PATCH * (2 if r == 0 else 1), 2 * HD), BF16) for r in range(4)],
        [SM] + [VM] * 3,
    )(jnp.stack([j, 1 + 2 * c]).astype(jnp.int32), stale_k, stale_v, scale_exps.T)
    arrived = [
        lax.ppermute(rounds[r], ("z", "yl", "yh", "c"), round_pairs(r)) for r in range(4)
    ]
    q, fresh_kv = call(
        fresh_layout_kernel,
        "fresh_layout",
        [shape((16, 2 * SUB, HD), BF16), shape((SUB, 2 * fresh_k.shape[1]), BF16)],
        [VM] * 3,
    )(fresh_q, fresh_k, fresh_v)
    arrived, q = lax.optimization_barrier((arrived, q))
    q = lax.all_to_all(q, "z", split_axis=0, concat_axis=0, tiled=True)

    shard = jnp.concatenate(arrived, axis=0)
    swap = [(0, 1), (1, 0)]
    parts = [shard] + [
        lax.ppermute(shard, ("yl", "yh"), [(i, i ^ k) for i in range(4)]) for k in (1, 2, 3)
    ]
    across_0 = lax.ppermute(shard, "c", swap)
    across_2 = lax.ppermute(parts[2], "c", swap)
    across_13 = lax.ppermute(jnp.concatenate([parts[1], parts[3]], axis=0), "c", swap)
    lows = []
    for core in (c, 1 - c):
        for k in range(4):
            source_yl, source_yh = yl ^ (k // 2), yh ^ (k % 2)
            move = source_yh ^ (z // 2 % 2)
            for r in range(4):
                patch = 4 * ((j + (4 - r) * (1 + 2 * (z % 2))) % 4) + 2 * (move ^ (z % 2)) + core
                lows.append(jnp.where(source_yl ^ move == yl, SUB * patch, -SUB))
    spans = jnp.stack([low.astype(jnp.int32) for low in lows])

    fresh_kv, parts[1], parts[3] = lax.optimization_barrier((fresh_kv, parts[1], parts[3]))
    fresh_far = lax.ppermute(fresh_kv, "yh", swap)
    rows = shard.shape[0]
    state = attend("keys_a", spans, q, [(shard, 0, 0), (across_0, 0, 16)])
    state = attend("keys_b", spans, q, [(parts[2], 0, 8), (across_2, 0, 24)], state)
    state = attend("keys_c", spans, q, [(parts[1], 0, 4), (parts[3], 0, 12)], state)
    (both,) = attend(
        "keys_d", spans, q, [(across_13, 0, 20), (across_13, rows, 28)], state, True
    )
    both = lax.all_to_all(both, "z", split_axis=0, concat_axis=0, tiled=True)

    fresh_two = jnp.concatenate([fresh_kv, fresh_far], axis=0)
    fresh, fresh_log = call(
        fresh_kernel,
        "own_patch",
        [shape(fresh_q.shape, F32), shape((SUB, HD), F32)],
        [VM] * 3,
    )(fresh_q, fresh_two, lax.ppermute(fresh_two, "c", [(0, 1), (1, 0)]))

    (out,) = call(merge_kernel, "merge", [shape(fresh_q.shape, BF16)], [VM] * 3)(
        both, fresh, fresh_log
    )
    return out


def solution(mesh):
    devices = np.asarray(mesh.devices).reshape(4, 16, 2, 2, 2)
    fine = Mesh(devices, ("x", "z", "yl", "yh", "c"))
    tokens = P(("x", "z", "yl", "yh", "c"), None)
    stored = P(("x", "z", "yl"), ("yh", "c"))
    in_specs = (tokens, tokens, tokens, stored, stored, P(("x", "z", "yl"), None))
    return jax.shard_map(
        per_device, mesh=fine, in_specs=in_specs, out_specs=tokens, check_vma=False
    )
```

time: 480 us -> 137 us (0.29)
  the two profiles are of different devices: /device:TPU:1 before, /device:TPU:4 now
where the time goes in v2:
time: 137 us; the launch traced here: 136 us
  starting transfers between devices  75.3 us (55%)
  waiting for transfers between devices  29.5 us (22%)
  Pallas kernels  23 us (17%)
  local copies, waits for them, and re-layouts  6.73 us (5%)
    ppermute x4, starting transfers between devices, per_device(): lax.ppermute(rounds[r], ('z', 'yl', 'yh', 'c'), round_pairs(r))  26.1 us
    ppermute x3, starting transfers between devices, per_device(): lax.ppermute(shard, ('yl', 'yh'), [(i, i ^ k) for i in range(4)])  19 us
    all_to_all x1, waiting for transfers between devices, per_device(): both = lax.all_to_all(both, 'z', split_axis=0, concat_axis=0, tiled=True)  16 us
    pallas_call x4, Pallas kernels, attend(): return call(kernel, name, outs, specs)(spans, q, *arrays, *state)  14.7 us
    ppermute x3, waiting for transfers between devices, per_device(): lax.ppermute(shard, ('yl', 'yh'), [(i, i ^ k) for i in range(4)])  9.22 us
    all_to_all x1, starting transfers between devices, per_device(): both = lax.all_to_all(both, 'z', split_axis=0, concat_axis=0, tiled=True)  8.98 us
    all_to_all x1, starting transfers between devices, per_device(): q = lax.all_to_all(q, 'z', split_axis=0, concat_axis=0, tiled=True)  7.79 us
    unnamed x18, local copies, waits for them, and re-layouts  5.47 us
  transfers between devices with their start and end apart: 14, of which 5 were waited for; matrix products, arithmetic and copies ran while one was open for 2% of the time, Pallas kernels for 15%

profile of v2, /device:TPU:4, one launch (start us, length us, event | category | flops | bytes accessed | tf_op | source)
XLA Modules:
  0.0 136.1 jit_solution(9089768519142061248)
XLA Ops:
  0.1 0.9 copy-done.2
  1.0 0.9 copy-done.3
  2.6 0.8 stored_scaled.1
  4.2 9.1 %collective-permute-start.1 = (bf16[192,256]{1,0:T(8,128)(2,1)S(1)}, bf16[192,256]{1,0:T(8,128)(2,1)S(1)}, u32[]{:S(2)}, u32[]{:S(2)}) collective-permute-start(bf16[192,256]{1,0:T(8,128)(2,1)S(1)} %get-tuple-element.40), channel_id=1, source_target_pairs={{0,32},{1,110},{2,50},{3,124},{4,36},{5,106},{6,54},{7,120},{8,33}... | collective-permute-start | bytes 294920 | tf_op jit(solution)/shard_map/ppermute | solution.py:251
  13.3 10.9 %collective-permute-start.2 = (bf16[192,256]{1,0:T(8,128)(2,1)S(1)}, bf16[192,256]{1,0:T(8,128)(2,1)S(1)}, u32[]{:S(2)}, u32[]{:S(2)}) collective-permute-start(bf16[192,256]{1,0:T(8,128)(2,1)S(1)} %get-tuple-element.41), channel_id=1, source_target_pairs={{0,64},{1,78},{2,82},{3,92},{4,68},{5,74},{6,86},{7,88},{8,65},{9,... | collective-permute-start | bytes 294920 | tf_op jit(solution)/shard_map/ppermute | solution.py:251
  24.2 5.5 %collective-permute-start.3 = (bf16[192,256]{1,0:T(8,128)(2,1)S(1)}, bf16[192,256]{1,0:T(8,128)(2,1)S(1)}, u32[]{:S(2)}, u32[]{:S(2)}) collective-permute-start(bf16[192,256]{1,0:T(8,128)(2,1)S(1)} %get-tuple-element.42), channel_id=1, source_target_pairs={{0,96},{1,46},{2,114},{3,60},{4,100},{5,42},{6,118},{7,56},{8,97},... | collective-permute-start | bytes 294920 | tf_op jit(solution)/shard_map/ppermute | solution.py:251
  29.7 0.9 copy-done
  30.6 0.9 copy-done.4
  31.6 0.9 copy-done.5
  32.5 0.8 fresh_layout.1
  33.3 1.3 collective-permute-done.3
  34.8 13.1 %collective-permute-start.4 = (bf16[960,256]{1,0:T(8,128)(2,1)S(1)}, bf16[960,256]{1,0:T(8,128)(2,1)S(1)}, u32[]{:S(2)}, u32[]{:S(2)}) collective-permute-start(bf16[960,256]{1,0:T(8,128)(2,1)S(1)} %constant_dynamic-update-slice_fusion.refs_0_), channel_id=1, source_target_pairs={{0,2},{2,0},{4,6},{6,4},{1,3},{3,1},{5,7},{7,5},{8,10},{10,8},{12,... | collective-permute-start | bytes 1474568 | tf_op jit(solution)/shard_map/ppermute | solution.py:265
  47.9 3.3 %collective-permute-start.5 = (bf16[960,256]{1,0:T(8,128)(2,1)S(1)}, bf16[960,256]{1,0:T(8,128)(2,1)S(1)}, u32[]{:S(2)}, u32[]{:S(2)}) collective-permute-start(bf16[960,256]{1,0:T(8,128)(2,1)S(1)} %constant_dynamic-update-slice_fusion.refs_0_), channel_id=1, source_target_pairs={{0,6},{2,4},{4,2},{6,0},{1,7},{3,5},{5,3},{7,1},{8,14},{10,12},{12... | collective-permute-start | bytes 1474568 | tf_op jit(solution)/shard_map/ppermute | solution.py:265
  51.2 7.8 %all-to-all-start = ((bf16[16,96,128]{2,1,0:T(8,128)(2,1)}), bf16[16,96,128]{2,1,0:T(8,128)(2,1)S(1)}, u32[]{:S(2)}, u32[]{:S(2)}) async-start(bf16[16,96,128]{2,1,0:T(8,128)(2,1)} %get-tuple-element.44), calls=%async_computation | async-start | bytes 786432 | tf_op jit(solution)/shard_map/all_to_all | solution.py:260
  59.0 2.5 %collective-permute-start.7 = (bf16[960,256]{1,0:T(8,128)(2,1)S(1)}, bf16[960,256]{1,0:T(8,128)(2,1)}, u32[]{:S(2)}, u32[]{:S(2)}) collective-permute-start(bf16[960,256]{1,0:T(8,128)(2,1)S(1)} %constant_dynamic-update-slice_fusion.refs_0_), channel_id=1, source_target_pairs={{0,4},{2,6},{4,0},{6,2},{1,5},{3,7},{5,1},{7,3},{8,12},{10,14},{12... | collective-permute-start | bytes 1474568 | tf_op jit(solution)/shard_map/ppermute | solution.py:265
  61.6 9.2 %collective-permute-done.5.refs_1_ = bf16[960,256]{1,0:T(8,128)(2,1)S(1)} collective-permute-done((bf16[960,256]{1,0:T(8,128)(2,1)S(1)}, bf16[960,256]{1,0:T(8,128)(2,1)S(1)}, u32[]{:S(2)}, u32[]{:S(2)}) %collective-permute-start.5) | collective-permute-done | bytes 491552 | tf_op jit(solution)/shard_map/ppermute | solution.py:265
  70.8 1.0 pad_maximum_fusion
  71.8 1.9 %collective-permute-start.6 = (bf16[1920,256]{1,0:T(8,128)(2,1)}, bf16[1920,256]{1,0:T(8,128)(2,1)S(1)}, u32[]{:S(2)}, u32[]{:S(2)}) collective-permute-start(bf16[1920,256]{1,0:T(8,128)(2,1)} %pad_maximum_fusion), channel_id=1, source_target_pairs={{0,1},{1,0},{2,3},{3,2},{4,5},{5,4},{6,7},{7,6},{8,9},{9,8},{10,11... | collective-permute-start | bytes 2949128 | tf_op jit(solution)/shard_map/ppermute | solution.py:269
  73.8 2.4 %collective-permute-start.9 = (bf16[960,256]{1,0:T(8,128)(2,1)S(1)}, bf16[960,256]{1,0:T(8,128)(2,1)}, u32[]{:S(2)}, u32[]{:S(2)}) collective-permute-start(bf16[960,256]{1,0:T(8,128)(2,1)S(1)} %constant_dynamic-update-slice_fusion.refs_0_), channel_id=1, source_target_pairs={{0,1},{1,0},{2,3},{3,2},{4,5},{5,4},{6,7},{7,6},{8,9},{9,8},{10,11... | collective-permute-start | bytes 1474568 | tf_op jit(solution)/shard_map/ppermute | solution.py:267
  76.2 1.9 %collective-permute-start.8 = (bf16[960,256]{1,0:T(8,128)(2,1)}, bf16[960,256]{1,0:T(8,128)(2,1)}, u32[]{:S(2)}, u32[]{:S(2)}) collective-permute-start(bf16[960,256]{1,0:T(8,128)(2,1)} %collective-permute-done.7.refs_0_), channel_id=1, source_target_pairs={{0,1},{1,0},{2,3},{3,2},{4,5},{5,4},{6,7},{7,6},{8,9},{9,8},{10,11... | collective-permute-start | bytes 1474568 | tf_op jit(solution)/shard_map/ppermute | solution.py:268
  78.5 5.2 %collective-permute-start.10 = (bf16[48,5120]{1,0:T(8,128)(2,1)S(1)}, bf16[48,5120]{1,0:T(8,128)(2,1)}, u32[]{:S(2)}, u32[]{:S(2)}) collective-permute-start(bf16[48,5120]{1,0:T(8,128)(2,1)S(1)} %get-tuple-element.70), channel_id=1, source_target_pairs={{0,2},{2,0},{1,3},{3,1},{4,6},{6,4},{5,7},{7,5},{8,10},{10,8},{9,1... | collective-permute-start | bytes 1474568 | tf_op jit(solution)/shard_map/ppermute | solution.py:281
  84.1 3.1 %keys_a.1 = (f32[1,768]{1,0:T(1,128)S(1)}, f32[1,768]{1,0:T(1,128)S(1)}, f32[128,768]{1,0:T(8,128)S(1)}, f32[1,768]{1,0:T(1,128)S(1)}, f32[1,768]{1,0:T(1,128)S(1)}, /*index=5*/f32[128,768]{1,0:T(8,128)S(1)}) custom-call(s32[32]{0:T(128)S(1)} %stack.140.spans_ref, bf16[16,96,128]{2,1,0:T(8,128)(2,1)S(1)} %all-to-all-done.q_ref, ...), custom_call_target="tpu_custom_call" | custom-call | tf_op jit(solution)/shard_map/keys_a/pallas_call | solution.py:166
  87.2 3.9 %keys_b.1 = (f32[1,768]{1,0:T(1,128)S(1)}, f32[1,768]{1,0:T(1,128)S(1)}, f32[128,768]{1,0:T(8,128)S(1)}, f32[1,768]{1,0:T(1,128)S(1)}, f32[1,768]{1,0:T(1,128)S(1)}, /*index=5*/f32[128,768]{1,0:T(8,128)S(1)}) custom-call(s32[32]{0:T(128)S(1)} %stack.140.spans_ref, bf16[16,96,128]{2,1,0:T(8,128)(2,1)S(1)} %all-to-all-done.q_ref, ...), custom_call_target="tpu_custom_call" | custom-call | tf_op jit(solution)/shard_map/keys_b/pallas_call | solution.py:166
  91.1 3.3 %keys_c.1 = (f32[1,768]{1,0:T(1,128)S(1)}, f32[1,768]{1,0:T(1,128)S(1)}, f32[128,768]{1,0:T(8,128)S(1)}, f32[1,768]{1,0:T(1,128)S(1)}, f32[1,768]{1,0:T(1,128)S(1)}, /*index=5*/f32[128,768]{1,0:T(8,128)S(1)}) custom-call(s32[32]{0:T(128)S(1)} %stack.140.spans_ref, bf16[16,96,128]{2,1,0:T(8,128)(2,1)S(1)} %all-to-all-done.q_ref, ...), custom_call_target="tpu_custom_call" | custom-call | tf_op jit(solution)/shard_map/keys_c/pallas_call | solution.py:166
  94.4 4.4 %keys_d.1 = bf16[16,112,128]{2,1,0:T(8,128)(2,1)} custom-call(s32[32]{0:T(128)S(1)} %stack.140.spans_ref, bf16[16,96,128]{2,1,0:T(8,128)(2,1)S(1)} %all-to-all-done.q_ref, bf16[1920,256]{1,0:T(8,128)(2,1)S(1)} %collective-permute-done.6.refs_0_, f32[1,768]{1,0:T(1,128)S(1)} %get-tuple-element.64.refs_1_, f32[1,768]{1,0:T(1,128)S(1)} %get-tuple-element.65.refs_2_, ...), custom_call_target="tpu_custom_call" | custom-call | tf_op jit(solution)/shard_map/keys_d/pallas_call | solution.py:166
  98.8 9.0 %all-to-all-start.1 = ((bf16[16,112,128]{2,1,0:T(8,128)(2,1)}), bf16[16,112,128]{2,1,0:T(8,128)(2,1)S(1)}, u32[]{:S(2)}, u32[]{:S(2)}) async-start(bf16[16,112,128]{2,1,0:T(8,128)(2,1)} %keys_d.1), calls=%async_computation.1 | async-start | bytes 917504 | tf_op jit(solution)/shard_map/all_to_all | solution.py:289
  107.9 1.1 constant_dynamic-update-slice_fusion.4.near_ref
  109.0 1.9 %collective-permute-start.11 = (bf16[96,5120]{1,0:T(8,128)(2,1)S(1)}, bf16[96,5120]{1,0:T(8,128)(2,1)S(1)}, u32[]{:S(2)}, u32[]{:S(2)}) collective-permute-start(bf16[96,5120]{1,0:T(8,128)(2,1)S(1)} %constant_dynamic-update-slice_fusion.4.near_ref), channel_id=1, source_target_pairs={{0,1},{1,0},{2,3},{3,2},{4,5},{5,4},{6,7},{7,6},{8,9},{9,8},{10,11... | collective-permute-start | bytes 2949128 | tf_op jit(solution)/shard_map/ppermute | solution.py:297
  111.0 2.5 %collective-permute-done.11.far_ref = bf16[96,5120]{1,0:T(8,128)(2,1)S(1)} collective-permute-done((bf16[96,5120]{1,0:T(8,128)(2,1)S(1)}, bf16[96,5120]{1,0:T(8,128)(2,1)S(1)}, u32[]{:S(2)}, u32[]{:S(2)}) %collective-permute-start.11) | collective-permute-done | bytes 983072 | tf_op jit(solution)/shard_map/ppermute | solution.py:297
  113.5 5.2 %own_patch.1 = (f32[48,2560]{1,0:T(8,128)S(1)}, f32[48,128]{1,0:T(8,128)S(1)}) custom-call(bf16[48,2560]{1,0:T(8,128)(2,1)S(1)} %copy-done.1, bf16[96,5120]{1,0:T(8,128)(2,1)S(1)} %constant_dynamic-update-slice_fusion.4.near_ref, bf16[96,5120]{1,0:T(8,128)(2,1)S(1)} %collective-permute-done.11.far_ref), custom_call_target="tpu_custom_call" | custom-call | tf_op jit(solution)/shard_map/own_patch/pallas_call | solution.py:292
  118.7 16.0 %all-to-all-done.1.both_ref = bf16[16,112,128]{2,1,0:T(8,128)(2,1)S(1)} async-done(((bf16[16,112,128]{2,1,0:T(8,128)(2,1)}), bf16[16,112,128]{2,1,0:T(8,128)(2,1)S(1)}, u32[]{:S(2)}, u32[]{:S(2)}) %all-to-all-start.1) | async-done | bytes 458784 | tf_op jit(solution)/shard_map/all_to_all | solution.py:289
  134.7 1.4 %merge.1 = bf16[48,2560]{1,0:T(8,128)(2,1)} custom-call(bf16[16,112,128]{2,1,0:T(8,128)(2,1)S(1)} %all-to-all-done.1.both_ref, f32[48,2560]{1,0:T(8,128)S(1)} %get-tuple-element.71.fresh_ref, f32[48,128]{1,0:T(8,128)S(1)} %get-tuple-element.72.fresh_log_ref), custom_call_target="tpu_custom_call" | custom-call | tf_op jit(solution)/shard_map/merge/pallas_call | solution.py:299
  (27 shorter events, 2.0 us)
Async XLA Ops:
  0.1 0.9 copy-start.2
  1.0 0.9 copy-start.3
  2.0 0.7 copy-start.6
  3.5 31.2 %collective-permute-start = (bf16[384,256]{1,0:T(8,128)(2,1)S(1)}, bf16[384,256]{1,0:T(8,128)(2,1)S(1)}, u32[]{:S(2)}, u32[]{:S(2)}) collective-permute-start(bf16[384,256]{1,0:T(8,128)(2,1)S(1)} %get-tuple-element.39), channel_id=1, source_target_pairs={{0,0},{1,14},{2,18},{3,28},{4,4},{5,10},{6,22},{7,24},{8,1},{9,15}... | collective-permute-start | bytes 589832 | tf_op jit(solution)/shard_map/ppermute | solution.py:251
  4.2 29.2 %collective-permute-start.1 = (bf16[192,256]{1,0:T(8,128)(2,1)S(1)}, bf16[192,256]{1,0:T(8,128)(2,1)S(1)}, u32[]{:S(2)}, u32[]{:S(2)}) collective-permute-start(bf16[192,256]{1,0:T(8,128)(2,1)S(1)} %get-tuple-element.40), channel_id=1, source_target_pairs={{0,32},{1,110},{2,50},{3,124},{4,36},{5,106},{6,54},{7,120},{8,33}... | collective-permute-start | bytes 294920 | tf_op jit(solution)/shard_map/ppermute | solution.py:251
  13.3 20.1 %collective-permute-start.2 = (bf16[192,256]{1,0:T(8,128)(2,1)S(1)}, bf16[192,256]{1,0:T(8,128)(2,1)S(1)}, u32[]{:S(2)}, u32[]{:S(2)}) collective-permute-start(bf16[192,256]{1,0:T(8,128)(2,1)S(1)} %get-tuple-element.41), channel_id=1, source_target_pairs={{0,64},{1,78},{2,82},{3,92},{4,68},{5,74},{6,86},{7,88},{8,65},{9,... | collective-permute-start | bytes 294920 | tf_op jit(solution)/shard_map/ppermute | solution.py:251
  24.2 10.5 %collective-permute-start.3 = (bf16[192,256]{1,0:T(8,128)(2,1)S(1)}, bf16[192,256]{1,0:T(8,128)(2,1)S(1)}, u32[]{:S(2)}, u32[]{:S(2)}) collective-permute-start(bf16[192,256]{1,0:T(8,128)(2,1)S(1)} %get-tuple-element.42), channel_id=1, source_target_pairs={{0,96},{1,46},{2,114},{3,60},{4,100},{5,42},{6,118},{7,56},{8,97},... | collective-permute-start | bytes 294920 | tf_op jit(solution)/shard_map/ppermute | solution.py:251
  29.7 0.9 copy-start
  30.6 0.9 copy-start.4
  31.6 0.9 copy-start.5
  34.8 26.8 %collective-permute-start.4 = (bf16[960,256]{1,0:T(8,128)(2,1)S(1)}, bf16[960,256]{1,0:T(8,128)(2,1)S(1)}, u32[]{:S(2)}, u32[]{:S(2)}) collective-permute-start(bf16[960,256]{1,0:T(8,128)(2,1)S(1)} %constant_dynamic-update-slice_fusion.refs_0_), channel_id=1, source_target_pairs={{0,2},{2,0},{4,6},{6,4},{1,3},{3,1},{5,7},{7,5},{8,10},{10,8},{12,... | collective-permute-start | bytes 1474568 | tf_op jit(solution)/shard_map/ppermute | solution.py:265
  47.9 22.9 %collective-permute-start.5 = (bf16[960,256]{1,0:T(8,128)(2,1)S(1)}, bf16[960,256]{1,0:T(8,128)(2,1)S(1)}, u32[]{:S(2)}, u32[]{:S(2)}) collective-permute-start(bf16[960,256]{1,0:T(8,128)(2,1)S(1)} %constant_dynamic-update-slice_fusion.refs_0_), channel_id=1, source_target_pairs={{0,6},{2,4},{4,2},{6,0},{1,7},{3,5},{5,3},{7,1},{8,14},{10,12},{12... | collective-permute-start | bytes 1474568 | tf_op jit(solution)/shard_map/ppermute | solution.py:265
  51.2 32.9 %all-to-all-start = ((bf16[16,96,128]{2,1,0:T(8,128)(2,1)}), bf16[16,96,128]{2,1,0:T(8,128)(2,1)S(1)}, u32[]{:S(2)}, u32[]{:S(2)}) async-start(bf16[16,96,128]{2,1,0:T(8,128)(2,1)} %get-tuple-element.44), calls=%async_computation | async-start | bytes 786432 | tf_op jit(solution)/shard_map/all_to_all | solution.py:260
  59.0 17.1 %collective-permute-start.7 = (bf16[960,256]{1,0:T(8,128)(2,1)S(1)}, bf16[960,256]{1,0:T(8,128)(2,1)}, u32[]{:S(2)}, u32[]{:S(2)}) collective-permute-start(bf16[960,256]{1,0:T(8,128)(2,1)S(1)} %constant_dynamic-update-slice_fusion.refs_0_), channel_id=1, source_target_pairs={{0,4},{2,6},{4,0},{6,2},{1,5},{3,7},{5,1},{7,3},{8,12},{10,14},{12... | collective-permute-start | bytes 1474568 | tf_op jit(solution)/shard_map/ppermute | solution.py:265
  71.8 22.6 %collective-permute-start.6 = (bf16[1920,256]{1,0:T(8,128)(2,1)}, bf16[1920,256]{1,0:T(8,128)(2,1)S(1)}, u32[]{:S(2)}, u32[]{:S(2)}) collective-permute-start(bf16[1920,256]{1,0:T(8,128)(2,1)} %pad_maximum_fusion), channel_id=1, source_target_pairs={{0,1},{1,0},{2,3},{3,2},{4,5},{5,4},{6,7},{7,6},{8,9},{9,8},{10,11... | collective-permute-start | bytes 2949128 | tf_op jit(solution)/shard_map/ppermute | solution.py:269
  73.8 10.0 %collective-permute-start.9 = (bf16[960,256]{1,0:T(8,128)(2,1)S(1)}, bf16[960,256]{1,0:T(8,128)(2,1)}, u32[]{:S(2)}, u32[]{:S(2)}) collective-permute-start(bf16[960,256]{1,0:T(8,128)(2,1)S(1)} %constant_dynamic-update-slice_fusion.refs_0_), channel_id=1, source_target_pairs={{0,1},{1,0},{2,3},{3,2},{4,5},{5,4},{6,7},{7,6},{8,9},{9,8},{10,11... | collective-permute-start | bytes 1474568 | tf_op jit(solution)/shard_map/ppermute | solution.py:267
  76.2 11.0 %collective-permute-start.8 = (bf16[960,256]{1,0:T(8,128)(2,1)}, bf16[960,256]{1,0:T(8,128)(2,1)}, u32[]{:S(2)}, u32[]{:S(2)}) collective-permute-start(bf16[960,256]{1,0:T(8,128)(2,1)} %collective-permute-done.7.refs_0_), channel_id=1, source_target_pairs={{0,1},{1,0},{2,3},{3,2},{4,5},{5,4},{6,7},{7,6},{8,9},{9,8},{10,11... | collective-permute-start | bytes 1474568 | tf_op jit(solution)/shard_map/ppermute | solution.py:268
  78.5 29.4 %collective-permute-start.10 = (bf16[48,5120]{1,0:T(8,128)(2,1)S(1)}, bf16[48,5120]{1,0:T(8,128)(2,1)}, u32[]{:S(2)}, u32[]{:S(2)}) collective-permute-start(bf16[48,5120]{1,0:T(8,128)(2,1)S(1)} %get-tuple-element.70), channel_id=1, source_target_pairs={{0,2},{2,0},{1,3},{3,1},{4,6},{6,4},{5,7},{7,5},{8,10},{10,8},{9,1... | collective-permute-start | bytes 1474568 | tf_op jit(solution)/shard_map/ppermute | solution.py:281
  98.8 35.9 %all-to-all-start.1 = ((bf16[16,112,128]{2,1,0:T(8,128)(2,1)}), bf16[16,112,128]{2,1,0:T(8,128)(2,1)S(1)}, u32[]{:S(2)}, u32[]{:S(2)}) async-start(bf16[16,112,128]{2,1,0:T(8,128)(2,1)} %keys_d.1), calls=%async_computation.1 | async-start | bytes 917504 | tf_op jit(solution)/shard_map/all_to_all | solution.py:289
  107.8 5.6 %copy-start.1 = (bf16[48,2560]{1,0:T(8,128)(2,1)S(1)}, bf16[48,2560]{1,0:T(8,128)(2,1)}, u32[]{:S(2)}) copy-start(bf16[48,2560]{1,0:T(8,128)(2,1)} %q_ref.3) | copy-start | bytes 737284
  109.0 4.5 %collective-permute-start.11 = (bf16[96,5120]{1,0:T(8,128)(2,1)S(1)}, bf16[96,5120]{1,0:T(8,128)(2,1)S(1)}, u32[]{:S(2)}, u32[]{:S(2)}) collective-permute-start(bf16[96,5120]{1,0:T(8,128)(2,1)S(1)} %constant_dynamic-update-slice_fusion.4.near_ref), channel_id=1, source_target_pairs={{0,1},{1,0},{2,3},{3,2},{4,5},{5,4},{6,7},{7,6},{8,9},{9,8},{10,11... | collective-permute-start | bytes 2949128 | tf_op jit(solution)/shard_map/ppermute | solution.py:297

commit v3 on v2

--- a/solution.py
+++ b/solution.py
@@ -108,7 +108,7 @@
     log_sum = top * LOG2_SCALE + jnp.log2(total)
     high = log_sum.astype(BF16).astype(F32)
     middle = (log_sum - high).astype(BF16).astype(F32)
-    return (acc / total).T.astype(BF16), [high, middle, log_sum - high - middle]
+    return (acc * (1.0 / total)).T.astype(BF16), [high, middle, log_sum - high - middle]
 
 
 def queries_of(q_ref):
@@ -136,12 +136,17 @@
         return
     out_ref = refs[-1]
     count = results[0].shape[0]
-    rows = jnp.concatenate(rows + [jnp.zeros((10, count), F32)], axis=0)
+    rows = jnp.concatenate(rows + [jnp.zeros((2, count), F32)], axis=0)
+    empty = jnp.zeros((8, HD), F32)
     for n in range(count // SUB):
         out_ref[n, :SUB] = results[0][n * SUB : (n + 1) * SUB]
         out_ref[n, SUB : 2 * SUB] = results[1][n * SUB : (n + 1) * SUB]
-        moved = rows if n == 0 else pltpu.roll(rows, count - n * SUB, 1)
-        out_ref[n, 2 * SUB :] = moved[:, :HD].astype(BF16)
+        low = min(n * SUB // HD * HD, count - 2 * HD)
+        moved = rows[:, low : low + 2 * HD]
+        if n * SUB > low:
+            moved = pltpu.roll(moved, 2 * HD - (n * SUB - low), 1)
+        moved = jnp.concatenate([moved[:, :HD], empty], axis=0)
+        out_ref[n, 2 * SUB :] = moved.astype(BF16)
 
 
 def attend(name, spans, q, shards, state=None, last=False):
@@ -172,24 +177,36 @@
 
 
 def fresh_kernel(q_ref, near_ref, far_ref, out_ref, log_ref):
-    kv_refs = (near_ref, far_ref)
     width = q_ref.shape[1]
     lanes = lax.broadcasted_iota(jnp.int32, (SUB, HD), 1)
-    logs = jnp.zeros((SUB, HD), F32)
-    for h in range(width // HD):
-        at = h * HD
-        q = q_ref[:, at : at + HD]
-        k = jnp.concatenate([ref[:, at : at + HD] for ref in kv_refs], axis=0)
-        v = jnp.concatenate([ref[:, width + at : width + at + HD] for ref in kv_refs], axis=0)
-        s = lax.dot_general(q, k, (((1,), (1,)), ((), ())), preferred_element_type=F32)
-        top = jnp.max(s, axis=1, keepdims=True)
-        w = jnp.exp2((s - top) * LOG2_SCALE)
-        total = jnp.sum(w, axis=1, keepdims=True)
-        out_ref[:, at : at + HD] = (
-            jnp.dot(w.astype(BF16), v, preferred_element_type=F32) / total
-        )
-        logs = jnp.where(lanes == plane_order(h), top * LOG2_SCALE + jnp.log2(total), logs)
-    log_ref[...] = logs
+    tops, totals = jnp.zeros((SUB, HD), F32), jnp.ones((SUB, HD), F32)
+    both = (near_ref, far_ref)
+    for first in range(0, width // HD, 10):
+        heads = range(first, first + 10)
+        scores, weights = [], []
+        for h in heads:
+            at = h * HD
+            k = jnp.concatenate([ref[:, at : at + HD] for ref in both], axis=0)
+            scores.append(
+                lax.dot_general(
+                    q_ref[:, at : at + HD],
+                    k,
+                    (((1,), (1,)), ((), ())),
+                    preferred_element_type=F32,
+                )
+            )
+        peaks = [jnp.max(s, axis=1, keepdims=True) for s in scores]
+        for s, top in zip(scores, peaks):
+            weights.append(jnp.exp2((s - top) * LOG2_SCALE))
+        sums = [jnp.sum(w, axis=1, keepdims=True) for w in weights]
+        for h, w, top, total in zip(heads, weights, peaks, sums):
+            at = width + h * HD
+            v = jnp.concatenate([ref[:, at : at + HD] for ref in both], axis=0)
+            mixed = jnp.dot(w.astype(BF16), v, preferred_element_type=F32)
+            out_ref[:, h * HD : (h + 1) * HD] = mixed * (1.0 / total)
+            here = lanes == plane_order(h)
+            tops, totals = jnp.where(here, top, tops), jnp.where(here, total, totals)
+    log_ref[...] = tops * LOG2_SCALE + jnp.log2(totals)
 
 
 def merge_kernel(both_ref, fresh_ref, fresh_log_ref, out_ref):
@@ -277,15 +294,25 @@
                 lows.append(jnp.where(source_yl ^ move == yl, SUB * patch, -SUB))
     spans = jnp.stack([low.astype(jnp.int32) for low in lows])
 
-    fresh_kv, parts[1], parts[3] = lax.optimization_barrier((fresh_kv, parts[1], parts[3]))
+    rows = shard.shape[0]
+    state = attend(
+        "keys_first",
+        spans,
+        q,
+        [
+            (shard, 0, 0),
+            (across_0, 0, 16),
+            (parts[2], 0, 8),
+            (across_2, 0, 24),
+            (parts[1], 0, 4),
+            (parts[3], 0, 12),
+        ],
+    )
+    (both,) = attend(
+        "keys_last", spans, q, [(across_13, 0, 20), (across_13, rows, 28)], state, True
+    )
+    fresh_kv, both = lax.optimization_barrier((fresh_kv, both))
     fresh_far = lax.ppermute(fresh_kv, "yh", swap)
-    rows = shard.shape[0]
-    state = attend("keys_a", spans, q, [(shard, 0, 0), (across_0, 0, 16)])
-    state = attend("keys_b", spans, q, [(parts[2], 0, 8), (across_2, 0, 24)], state)
-    state = attend("keys_c", spans, q, [(parts[1], 0, 4), (parts[3], 0, 12)], state)
-    (both,) = attend(
-        "keys_d", spans, q, [(across_13, 0, 20), (across_13, rows, 28)], state, True
-    )
     both = lax.all_to_all(both, "z", split_axis=0, concat_axis=0, tiled=True)
 
     fresh_two = jnp.concatenate([fresh_kv, fresh_far], axis=0)

time: 137 us -> 131 us (0.956)
  the two profiles are of different devices: /device:TPU:4 before, /device:TPU:2 now
where the time goes in v3:
time: 131 us; the launch traced here: 130 us
  starting transfers between devices  72 us (55%)
  waiting for transfers between devices  35.3 us (27%)
  Pallas kernels  15.4 us (12%)
  local copies, waits for them, and re-layouts  5.65 us (4%)
    ppermute x4, starting transfers between devices, per_device(): lax.ppermute(rounds[r], ('z', 'yl', 'yh', 'c'), round_pairs(r))  26.1 us
    ppermute x3, starting transfers between devices, per_device(): lax.ppermute(shard, ('yl', 'yh'), [(i, i ^ k) for i in range(4)])  20.2 us
    ppermute x1, waiting for transfers between devices, per_device(): fresh_far = lax.ppermute(fresh_kv, 'yh', swap)  11.4 us
    pallas_call x2, Pallas kernels, attend(): return call(kernel, name, outs, specs)(spans, q, *arrays, *state)  11.1 us
    ppermute x3, waiting for transfers between devices, per_device(): lax.ppermute(shard, ('yl', 'yh'), [(i, i ^ k) for i in range(4)])  9.08 us
    all_to_all x1, starting transfers between devices, per_device(): q = lax.all_to_all(q, 'z', split_axis=0, concat_axis=0, tiled=True)  7.19 us
    unnamed x18, local copies, waits for them, and re-layouts  5.47 us
    all_to_all x1, starting transfers between devices, per_device(): both = lax.all_to_all(both, 'z', split_axis=0, concat_axis=0, tiled=True)  5.19 us
  transfers between devices with their start and end apart: 14, of which 7 were waited for; matrix products, arithmetic and copies ran while one was open for 1% of the time, Pallas kernels for 7%

profile of v3, /device:TPU:2, one launch (start us, length us, event | category | flops | bytes accessed | tf_op | source)
XLA Modules:
  0.0 129.9 jit_solution(14705720827237528843)
XLA Ops:
  0.1 0.9 copy-done.2
  1.0 0.9 copy-done.3
  2.6 0.8 stored_scaled.1
  4.2 9.1 %collective-permute-start.1 = (bf16[192,256]{1,0:T(8,128)(2,1)S(1)}, bf16[192,256]{1,0:T(8,128)(2,1)S(1)}, u32[]{:S(2)}, u32[]{:S(2)}) collective-permute-start(bf16[192,256]{1,0:T(8,128)(2,1)S(1)} %get-tuple-element.28), channel_id=1, source_target_pairs={{0,32},{1,110},{2,50},{3,124},{4,36},{5,106},{6,54},{7,120},{8,33}... | collective-permute-start | bytes 294920 | tf_op jit(solution)/shard_map/ppermute | solution.py:268
  13.3 10.9 %collective-permute-start.2 = (bf16[192,256]{1,0:T(8,128)(2,1)S(1)}, bf16[192,256]{1,0:T(8,128)(2,1)S(1)}, u32[]{:S(2)}, u32[]{:S(2)}) collective-permute-start(bf16[192,256]{1,0:T(8,128)(2,1)S(1)} %get-tuple-element.29), channel_id=1, source_target_pairs={{0,64},{1,78},{2,82},{3,92},{4,68},{5,74},{6,86},{7,88},{8,65},{9,... | collective-permute-start | bytes 294920 | tf_op jit(solution)/shard_map/ppermute | solution.py:268
  24.2 5.5 %collective-permute-start.3 = (bf16[192,256]{1,0:T(8,128)(2,1)S(1)}, bf16[192,256]{1,0:T(8,128)(2,1)S(1)}, u32[]{:S(2)}, u32[]{:S(2)}) collective-permute-start(bf16[192,256]{1,0:T(8,128)(2,1)S(1)} %get-tuple-element.30), channel_id=1, source_target_pairs={{0,96},{1,46},{2,114},{3,60},{4,100},{5,42},{6,118},{7,56},{8,97},... | collective-permute-start | bytes 294920 | tf_op jit(solution)/shard_map/ppermute | solution.py:268
  29.7 0.9 copy-done
  30.6 0.9 copy-done.4
  31.6 0.9 copy-done.5
  32.5 0.8 fresh_layout.1
  33.3 1.3 %collective-permute-done.3 = bf16[192,256]{1,0:T(8,128)(2,1)S(1)} collective-permute-done((bf16[192,256]{1,0:T(8,128)(2,1)S(1)}, bf16[192,256]{1,0:T(8,128)(2,1)S(1)}, u32[]{:S(2)}, u32[]{:S(2)}) %collective-permute-start.3) | collective-permute-done | bytes 98336 | tf_op jit(solution)/shard_map/ppermute | solution.py:268
  34.8 14.5 %collective-permute-start.5 = (bf16[960,256]{1,0:T(8,128)(2,1)S(1)}, bf16[960,256]{1,0:T(8,128)(2,1)S(1)}, u32[]{:S(2)}, u32[]{:S(2)}) collective-permute-start(bf16[960,256]{1,0:T(8,128)(2,1)S(1)} %constant_dynamic-update-slice_fusion.refs_0_), channel_id=1, source_target_pairs={{0,6},{2,4},{4,2},{6,0},{1,7},{3,5},{5,3},{7,1},{8,14},{10,12},{12... | collective-permute-start | bytes 1474568 | tf_op jit(solution)/shard_map/ppermute | solution.py:282
  49.3 1.9 %collective-permute-start.4 = (bf16[960,256]{1,0:T(8,128)(2,1)S(1)}, bf16[960,256]{1,0:T(8,128)(2,1)S(1)}, u32[]{:S(2)}, u32[]{:S(2)}) collective-permute-start(bf16[960,256]{1,0:T(8,128)(2,1)S(1)} %constant_dynamic-update-slice_fusion.refs_0_), channel_id=1, source_target_pairs={{0,2},{2,0},{4,6},{6,4},{1,3},{3,1},{5,7},{7,5},{8,10},{10,8},{12,... | collective-permute-start | bytes 1474568 | tf_op jit(solution)/shard_map/ppermute | solution.py:282
  51.2 7.2 %all-to-all-start = ((bf16[16,96,128]{2,1,0:T(8,128)(2,1)}), bf16[16,96,128]{2,1,0:T(8,128)(2,1)S(1)}, u32[]{:S(2)}, u32[]{:S(2)}) async-start(bf16[16,96,128]{2,1,0:T(8,128)(2,1)} %get-tuple-element.32), calls=%async_computation | async-start | bytes 786432 | tf_op jit(solution)/shard_map/all_to_all | solution.py:277
  58.4 3.7 %collective-permute-start.8 = (bf16[960,256]{1,0:T(8,128)(2,1)S(1)}, bf16[960,256]{1,0:T(8,128)(2,1)}, u32[]{:S(2)}, u32[]{:S(2)}) collective-permute-start(bf16[960,256]{1,0:T(8,128)(2,1)S(1)} %constant_dynamic-update-slice_fusion.refs_0_), channel_id=1, source_target_pairs={{0,4},{2,6},{4,0},{6,2},{1,5},{3,7},{5,1},{7,3},{8,12},{10,14},{12... | collective-permute-start | bytes 1474568 | tf_op jit(solution)/shard_map/ppermute | solution.py:282
  62.2 9.1 %collective-permute-done.5.refs_5_ = bf16[960,256]{1,0:T(8,128)(2,1)S(1)} collective-permute-done((bf16[960,256]{1,0:T(8,128)(2,1)S(1)}, bf16[960,256]{1,0:T(8,128)(2,1)S(1)}, u32[]{:S(2)}, u32[]{:S(2)}) %collective-permute-start.5) | collective-permute-done | bytes 491552 | tf_op jit(solution)/shard_map/ppermute | solution.py:282
  71.3 1.0 pad_maximum_fusion
  72.3 1.9 %collective-permute-start.6 = (bf16[1920,256]{1,0:T(8,128)(2,1)}, bf16[1920,256]{1,0:T(8,128)(2,1)S(1)}, u32[]{:S(2)}, u32[]{:S(2)}) collective-permute-start(bf16[1920,256]{1,0:T(8,128)(2,1)} %pad_maximum_fusion), channel_id=1, source_target_pairs={{0,1},{1,0},{2,3},{3,2},{4,5},{5,4},{6,7},{7,6},{8,9},{9,8},{10,11... | collective-permute-start | bytes 2949128 | tf_op jit(solution)/shard_map/ppermute | solution.py:286
  74.2 2.4 %collective-permute-start.7 = (bf16[960,256]{1,0:T(8,128)(2,1)S(1)}, bf16[960,256]{1,0:T(8,128)(2,1)}, u32[]{:S(2)}, u32[]{:S(2)}) collective-permute-start(bf16[960,256]{1,0:T(8,128)(2,1)S(1)} %constant_dynamic-update-slice_fusion.refs_0_), channel_id=1, source_target_pairs={{0,1},{1,0},{2,3},{3,2},{4,5},{5,4},{6,7},{7,6},{8,9},{9,8},{10,11... | collective-permute-start | bytes 1474568 | tf_op jit(solution)/shard_map/ppermute | solution.py:284
  76.6 1.9 %collective-permute-start.9 = (bf16[960,256]{1,0:T(8,128)(2,1)}, bf16[960,256]{1,0:T(8,128)(2,1)}, u32[]{:S(2)}, u32[]{:S(2)}) collective-permute-start(bf16[960,256]{1,0:T(8,128)(2,1)} %collective-permute-done.8.refs_2_), channel_id=1, source_target_pairs={{0,1},{1,0},{2,3},{3,2},{4,5},{5,4},{6,7},{7,6},{8,9},{9,8},{10,11... | collective-permute-start | bytes 1474568 | tf_op jit(solution)/shard_map/ppermute | solution.py:285
  78.9 1.8 %collective-permute-done.9.refs_3_ = bf16[960,256]{1,0:T(8,128)(2,1)} collective-permute-done((bf16[960,256]{1,0:T(8,128)(2,1)}, bf16[960,256]{1,0:T(8,128)(2,1)}, u32[]{:S(2)}, u32[]{:S(2)}) %collective-permute-start.9) | collective-permute-done | bytes 491552 | tf_op jit(solution)/shard_map/ppermute | solution.py:285
  80.7 4.4 %all-to-all-done.q_ref = bf16[16,96,128]{2,1,0:T(8,128)(2,1)S(1)} async-done(((bf16[16,96,128]{2,1,0:T(8,128)(2,1)}), bf16[16,96,128]{2,1,0:T(8,128)(2,1)S(1)}, u32[]{:S(2)}, u32[]{:S(2)}) %all-to-all-start) | async-done | bytes 393248 | tf_op jit(solution)/shard_map/all_to_all | solution.py:277
  85.2 6.7 %keys_first.1 = (f32[1,768]{1,0:T(1,128)S(1)}, f32[1,768]{1,0:T(1,128)S(1)}, f32[128,768]{1,0:T(8,128)S(1)}, f32[1,768]{1,0:T(1,128)S(1)}, f32[1,768]{1,0:T(1,128)S(1)}, /*index=5*/f32[128,768]{1,0:T(8,128)S(1)}) custom-call(s32[32]{0:T(128)S(1)} %stack.140.spans_ref, bf16[16,96,128]{2,1,0:T(8,128)(2,1)S(1)} %all-to-all-done.q_ref, ...), custom_call_target="tpu_custom_call" | custom-call | tf_op jit(solution)/shard_map/keys_first/pallas_call | solution.py:171
  91.9 4.4 %keys_last.1 = bf16[16,112,128]{2,1,0:T(8,128)(2,1)} custom-call(s32[32]{0:T(128)S(1)} %stack.140.spans_ref, bf16[16,96,128]{2,1,0:T(8,128)(2,1)S(1)} %all-to-all-done.q_ref, bf16[1920,256]{1,0:T(8,128)(2,1)S(1)} %collective-permute-done.6.refs_0_, f32[1,768]{1,0:T(1,128)S(1)} %get-tuple-element.37.refs_1_, f32[1,768]{1,0:T(1,128)S(1)} %get-tuple-element.38.refs_2_, ...), custom_call_target="tpu_custom_call" | custom-call | tf_op jit(solution)/shard_map/keys_last/pallas_call | solution.py:171
  96.3 5.2 %all-to-all-start.1 = ((bf16[16,112,128]{2,1,0:T(8,128)(2,1)}), bf16[16,112,128]{2,1,0:T(8,128)(2,1)S(1)}, u32[]{:S(2)}, u32[]{:S(2)}) async-start(bf16[16,112,128]{2,1,0:T(8,128)(2,1)} %keys_last.1), calls=%async_computation.1 | async-start | bytes 917504 | tf_op jit(solution)/shard_map/all_to_all | solution.py:316
  101.5 5.1 %collective-permute-start.10 = (bf16[48,5120]{1,0:T(8,128)(2,1)S(1)}, bf16[48,5120]{1,0:T(8,128)(2,1)S(1)}, u32[]{:S(2)}, u32[]{:S(2)}) collective-permute-start(bf16[48,5120]{1,0:T(8,128)(2,1)S(1)} %get-tuple-element.44), channel_id=1, source_target_pairs={{0,2},{2,0},{1,3},{3,1},{4,6},{6,4},{5,7},{7,5},{8,10},{10,8},{9,1... | collective-permute-start | bytes 1474568 | tf_op jit(solution)/shard_map/ppermute | solution.py:315
  106.7 11.4 %collective-permute-done.10 = bf16[48,5120]{1,0:T(8,128)(2,1)S(1)} collective-permute-done((bf16[48,5120]{1,0:T(8,128)(2,1)S(1)}, bf16[48,5120]{1,0:T(8,128)(2,1)S(1)}, u32[]{:S(2)}, u32[]{:S(2)}) %collective-permute-start.10) | collective-permute-done | bytes 491552 | tf_op jit(solution)/shard_map/ppermute | solution.py:315
  118.1 1.9 %collective-permute-start.11 = (bf16[96,5120]{1,0:T(8,128)(2,1)S(1)}, bf16[96,5120]{1,0:T(8,128)(2,1)S(1)}, u32[]{:S(2)}, u32[]{:S(2)}) collective-permute-start(bf16[96,5120]{1,0:T(8,128)(2,1)S(1)} %constant_dynamic-update-slice_fusion.4.near_ref), channel_id=1, source_target_pairs={{0,1},{1,0},{2,3},{3,2},{4,5},{5,4},{6,7},{7,6},{8,9},{9,8},{10,11... | collective-permute-start | bytes 2949128 | tf_op jit(solution)/shard_map/ppermute | solution.py:324
  120.0 2.5 %collective-permute-done.11.far_ref = bf16[96,5120]{1,0:T(8,128)(2,1)S(1)} collective-permute-done((bf16[96,5120]{1,0:T(8,128)(2,1)S(1)}, bf16[96,5120]{1,0:T(8,128)(2,1)S(1)}, u32[]{:S(2)}, u32[]{:S(2)}) %collective-permute-start.11) | collective-permute-done | bytes 983072 | tf_op jit(solution)/shard_map/ppermute | solution.py:324
  122.5 1.2 own_patch.1
  123.8 4.7 %all-to-all-done.1.both_ref = bf16[16,112,128]{2,1,0:T(8,128)(2,1)S(1)} async-done(((bf16[16,112,128]{2,1,0:T(8,128)(2,1)}), bf16[16,112,128]{2,1,0:T(8,128)(2,1)S(1)}, u32[]{:S(2)}, u32[]{:S(2)}) %all-to-all-start.1) | async-done | bytes 458784 | tf_op jit(solution)/shard_map/all_to_all | solution.py:316
  128.5 1.4 %merge.1 = bf16[48,2560]{1,0:T(8,128)(2,1)} custom-call(bf16[16,112,128]{2,1,0:T(8,128)(2,1)S(1)} %all-to-all-done.1.both_ref, f32[48,2560]{1,0:T(8,128)S(1)} %get-tuple-element.45.fresh_ref, f32[48,128]{1,0:T(8,128)S(1)} %get-tuple-element.46.fresh_log_ref), custom_call_target="tpu_custom_call" | custom-call | tf_op jit(solution)/shard_map/merge/pallas_call | solution.py:326
  (25 shorter events, 1.7 us)
Async XLA Ops:
  0.1 0.9 copy-start.2
  1.0 0.9 copy-start.3
  2.0 0.7 copy-start.6
  3.5 31.2 %collective-permute-start = (bf16[384,256]{1,0:T(8,128)(2,1)S(1)}, bf16[384,256]{1,0:T(8,128)(2,1)S(1)}, u32[]{:S(2)}, u32[]{:S(2)}) collective-permute-start(bf16[384,256]{1,0:T(8,128)(2,1)S(1)} %get-tuple-element.27), channel_id=1, source_target_pairs={{0,0},{1,14},{2,18},{3,28},{4,4},{5,10},{6,22},{7,24},{8,1},{9,15}... | collective-permute-start | bytes 589832 | tf_op jit(solution)/shard_map/ppermute | solution.py:268
  4.2 29.2 %collective-permute-start.1 = (bf16[192,256]{1,0:T(8,128)(2,1)S(1)}, bf16[192,256]{1,0:T(8,128)(2,1)S(1)}, u32[]{:S(2)}, u32[]{:S(2)}) collective-permute-start(bf16[192,256]{1,0:T(8,128)(2,1)S(1)} %get-tuple-element.28), channel_id=1, source_target_pairs={{0,32},{1,110},{2,50},{3,124},{4,36},{5,106},{6,54},{7,120},{8,33}... | collective-permute-start | bytes 294920 | tf_op jit(solution)/shard_map/ppermute | solution.py:268
  13.3 20.1 %collective-permute-start.2 = (bf16[192,256]{1,0:T(8,128)(2,1)S(1)}, bf16[192,256]{1,0:T(8,128)(2,1)S(1)}, u32[]{:S(2)}, u32[]{:S(2)}) collective-permute-start(bf16[192,256]{1,0:T(8,128)(2,1)S(1)} %get-tuple-element.29), channel_id=1, source_target_pairs={{0,64},{1,78},{2,82},{3,92},{4,68},{5,74},{6,86},{7,88},{8,65},{9,... | collective-permute-start | bytes 294920 | tf_op jit(solution)/shard_map/ppermute | solution.py:268
  24.2 10.5 %collective-permute-start.3 = (bf16[192,256]{1,0:T(8,128)(2,1)S(1)}, bf16[192,256]{1,0:T(8,128)(2,1)S(1)}, u32[]{:S(2)}, u32[]{:S(2)}) collective-permute-start(bf16[192,256]{1,0:T(8,128)(2,1)S(1)} %get-tuple-element.30), channel_id=1, source_target_pairs={{0,96},{1,46},{2,114},{3,60},{4,100},{5,42},{6,118},{7,56},{8,97},... | collective-permute-start | bytes 294920 | tf_op jit(solution)/shard_map/ppermute | solution.py:268
  29.7 0.9 copy-start
  30.6 0.9 copy-start.4
  31.6 0.9 copy-start.5
  34.8 36.5 %collective-permute-start.5 = (bf16[960,256]{1,0:T(8,128)(2,1)S(1)}, bf16[960,256]{1,0:T(8,128)(2,1)S(1)}, u32[]{:S(2)}, u32[]{:S(2)}) collective-permute-start(bf16[960,256]{1,0:T(8,128)(2,1)S(1)} %constant_dynamic-update-slice_fusion.refs_0_), channel_id=1, source_target_pairs={{0,6},{2,4},{4,2},{6,0},{1,7},{3,5},{5,3},{7,1},{8,14},{10,12},{12... | collective-permute-start | bytes 1474568 | tf_op jit(solution)/shard_map/ppermute | solution.py:282
  49.3 21.9 %collective-permute-start.4 = (bf16[960,256]{1,0:T(8,128)(2,1)S(1)}, bf16[960,256]{1,0:T(8,128)(2,1)S(1)}, u32[]{:S(2)}, u32[]{:S(2)}) collective-permute-start(bf16[960,256]{1,0:T(8,128)(2,1)S(1)} %constant_dynamic-update-slice_fusion.refs_0_), channel_id=1, source_target_pairs={{0,2},{2,0},{4,6},{6,4},{1,3},{3,1},{5,7},{7,5},{8,10},{10,8},{12,... | collective-permute-start | bytes 1474568 | tf_op jit(solution)/shard_map/ppermute | solution.py:282
  51.2 33.9 %all-to-all-start = ((bf16[16,96,128]{2,1,0:T(8,128)(2,1)}), bf16[16,96,128]{2,1,0:T(8,128)(2,1)S(1)}, u32[]{:S(2)}, u32[]{:S(2)}) async-start(bf16[16,96,128]{2,1,0:T(8,128)(2,1)} %get-tuple-element.32), calls=%async_computation | async-start | bytes 786432 | tf_op jit(solution)/shard_map/all_to_all | solution.py:277
  58.4 18.2 %collective-permute-start.8 = (bf16[960,256]{1,0:T(8,128)(2,1)S(1)}, bf16[960,256]{1,0:T(8,128)(2,1)}, u32[]{:S(2)}, u32[]{:S(2)}) collective-permute-start(bf16[960,256]{1,0:T(8,128)(2,1)S(1)} %constant_dynamic-update-slice_fusion.refs_0_), channel_id=1, source_target_pairs={{0,4},{2,6},{4,0},{6,2},{1,5},{3,7},{5,1},{7,3},{8,12},{10,14},{12... | collective-permute-start | bytes 1474568 | tf_op jit(solution)/shard_map/ppermute | solution.py:282
  72.3 19.6 %collective-permute-start.6 = (bf16[1920,256]{1,0:T(8,128)(2,1)}, bf16[1920,256]{1,0:T(8,128)(2,1)S(1)}, u32[]{:S(2)}, u32[]{:S(2)}) collective-permute-start(bf16[1920,256]{1,0:T(8,128)(2,1)} %pad_maximum_fusion), channel_id=1, source_target_pairs={{0,1},{1,0},{2,3},{3,2},{4,5},{5,4},{6,7},{7,6},{8,9},{9,8},{10,11... | collective-permute-start | bytes 2949128 | tf_op jit(solution)/shard_map/ppermute | solution.py:286
  74.2 4.7 %collective-permute-start.7 = (bf16[960,256]{1,0:T(8,128)(2,1)S(1)}, bf16[960,256]{1,0:T(8,128)(2,1)}, u32[]{:S(2)}, u32[]{:S(2)}) collective-permute-start(bf16[960,256]{1,0:T(8,128)(2,1)S(1)} %constant_dynamic-update-slice_fusion.refs_0_), channel_id=1, source_target_pairs={{0,1},{1,0},{2,3},{3,2},{4,5},{5,4},{6,7},{7,6},{8,9},{9,8},{10,11... | collective-permute-start | bytes 1474568 | tf_op jit(solution)/shard_map/ppermute | solution.py:284
  76.6 4.1 %collective-permute-start.9 = (bf16[960,256]{1,0:T(8,128)(2,1)}, bf16[960,256]{1,0:T(8,128)(2,1)}, u32[]{:S(2)}, u32[]{:S(2)}) collective-permute-start(bf16[960,256]{1,0:T(8,128)(2,1)} %collective-permute-done.8.refs_2_), channel_id=1, source_target_pairs={{0,1},{1,0},{2,3},{3,2},{4,5},{5,4},{6,7},{7,6},{8,9},{9,8},{10,11... | collective-permute-start | bytes 1474568 | tf_op jit(solution)/shard_map/ppermute | solution.py:285
  96.3 32.2 %all-to-all-start.1 = ((bf16[16,112,128]{2,1,0:T(8,128)(2,1)}), bf16[16,112,128]{2,1,0:T(8,128)(2,1)S(1)}, u32[]{:S(2)}, u32[]{:S(2)}) async-start(bf16[16,112,128]{2,1,0:T(8,128)(2,1)} %keys_last.1), calls=%async_computation.1 | async-start | bytes 917504 | tf_op jit(solution)/shard_map/all_to_all | solution.py:316
  101.5 21.0 %copy-start.1 = (bf16[48,2560]{1,0:T(8,128)(2,1)S(1)}, bf16[48,2560]{1,0:T(8,128)(2,1)}, u32[]{:S(2)}) copy-start(bf16[48,2560]{1,0:T(8,128)(2,1)} %q_ref.3) | copy-start | bytes 737284
  101.5 16.5 %collective-permute-start.10 = (bf16[48,5120]{1,0:T(8,128)(2,1)S(1)}, bf16[48,5120]{1,0:T(8,128)(2,1)S(1)}, u32[]{:S(2)}, u32[]{:S(2)}) collective-permute-start(bf16[48,5120]{1,0:T(8,128)(2,1)S(1)} %get-tuple-element.44), channel_id=1, source_target_pairs={{0,2},{2,0},{1,3},{3,1},{4,6},{6,4},{5,7},{7,5},{8,10},{10,8},{9,1... | collective-permute-start | bytes 1474568 | tf_op jit(solution)/shard_map/ppermute | solution.py:315
  118.1 4.5 %collective-permute-start.11 = (bf16[96,5120]{1,0:T(8,128)(2,1)S(1)}, bf16[96,5120]{1,0:T(8,128)(2,1)S(1)}, u32[]{:S(2)}, u32[]{:S(2)}) collective-permute-start(bf16[96,5120]{1,0:T(8,128)(2,1)S(1)} %constant_dynamic-update-slice_fusion.4.near_ref), channel_id=1, source_target_pairs={{0,1},{1,0},{2,3},{3,2},{4,5},{5,4},{6,7},{7,6},{8,9},{9,8},{10,11... | collective-permute-start | bytes 2949128 | tf_op jit(solution)/shard_map/ppermute | solution.py:324

commit v4 on v3

--- a/solution.py
+++ b/solution.py
@@ -45,7 +45,7 @@
         ref[row : row + PATCH, HD:] = v.astype(BF16)
 
     for r in range(4):
-        j = (first_ref[0] + r * first_ref[1]) % 4
+        j = (first_ref[0] + r) % 4
         put(rounds[r], 0, pl.multiple_of(j * HD, HD))
     put(rounds[0], PATCH, 4 * HD)
 
@@ -159,7 +159,7 @@
         at = [n for n, other in enumerate(arrays) if other is array][0]
         main += [(at, row + (r + 1 if r else 0) * PATCH, span + r) for r in range(4)]
         extra.append((at, row + PATCH, span))
-    groups = ([main[n : n + 8] for n in range(0, len(main), 8)], [extra])
+    groups = ([main[n : n + 12] for n in range(0, len(main), 12)], [extra])
     count = q.shape[0] * SUB
     shape = jax.ShapeDtypeStruct
     outs = [shape((1, count), F32), shape((1, count), F32), shape((HD, count), F32)] * 2
@@ -247,7 +247,7 @@
             for yh in range(2):
                 for c in range(2):
                     g, move = yh * 2 + c, (z // 2 % 2) ^ c
-                    plane = 4 * ((z // 4 + (r if c == 0 else 4 - r)) % 4) + g
+                    plane = 4 * ((z // 4 + r) % 4) + g
                     target = ((plane * 2 + (yl ^ move)) * 2 + (yh ^ move)) * 2 + z % 2
                     pairs.append(((z * 2 + yl) * 4 + g, target))
     return pairs
@@ -263,7 +263,7 @@
         "stored_scaled",
         [shape((PATCH * (2 if r == 0 else 1), 2 * HD), BF16) for r in range(4)],
         [SM] + [VM] * 3,
-    )(jnp.stack([j, 1 + 2 * c]).astype(jnp.int32), stale_k, stale_v, scale_exps.T)
+    )(j.reshape(1).astype(jnp.int32), stale_k, stale_v, scale_exps.T)
     arrived = [
         lax.ppermute(rounds[r], ("z", "yl", "yh", "c"), round_pairs(r)) for r in range(4)
     ]
@@ -290,7 +290,7 @@
             source_yl, source_yh = yl ^ (k // 2), yh ^ (k % 2)
             move = source_yh ^ (z // 2 % 2)
             for r in range(4):
-                patch = 4 * ((j + (4 - r) * (1 + 2 * (z % 2))) % 4) + 2 * (move ^ (z % 2)) + core
+                patch = 4 * ((j + 4 - r) % 4) + 2 * (move ^ (z % 2)) + core
                 lows.append(jnp.where(source_yl ^ move == yl, SUB * patch, -SUB))
     spans = jnp.stack([low.astype(jnp.int32) for low in lows])
 

time: 131 us -> 130 us (level)
  the two profiles are of different devices: /device:TPU:2 before, /device:TPU:14 now
where the time goes in v4:
time: 130 us; the launch traced here: 129 us
  starting transfers between devices  73.4 us (56%)
  waiting for transfers between devices  33.5 us (26%)
  Pallas kernels  14.8 us (11%)
  local copies, waits for them, and re-layouts  5.65 us (4%)
    ppermute x4, starting transfers between devices, per_device(): lax.ppermute(rounds[r], ('z', 'yl', 'yh', 'c'), round_pairs(r))  26.1 us
    ppermute x3, starting transfers between devices, per_device(): lax.ppermute(shard, ('yl', 'yh'), [(i, i ^ k) for i in range(4)])  16.7 us
    ppermute x1, waiting for transfers between devices, per_device(): fresh_far = lax.ppermute(fresh_kv, 'yh', swap)  13.3 us
    pallas_call x2, Pallas kernels, attend(): return call(kernel, name, outs, specs)(spans, q, *arrays, *state)  11.1 us
    all_to_all x1, starting transfers between devices, per_device(): q = lax.all_to_all(q, 'z', split_axis=0, concat_axis=0, tiled=True)  10.9 us
    all_to_all x1, starting transfers between devices, per_device(): both = lax.all_to_all(both, 'z', split_axis=0, concat_axis=0, tiled=True)  8.27 us
    ppermute x3, waiting for transfers between devices, per_device(): lax.ppermute(shard, ('yl', 'yh'), [(i, i ^ k) for i in range(4)])  6.41 us
    unnamed x18, local copies, waits for them, and re-layouts  5.47 us
  transfers between devices with their start and end apart: 14, of which 7 were waited for; matrix products, arithmetic and copies ran while one was open for 1% of the time, Pallas kernels for 7%

profile of v4, /device:TPU:14, one launch (start us, length us, event | category | flops | bytes accessed | tf_op | source)
XLA Modules:
  0.0 128.9 jit_solution(947011349835090982)
XLA Ops:
  0.0 0.9 copy-done.2
  0.9 0.9 copy-done.3
  1.9 0.7 copy-done.6
  3.5 9.1 %collective-permute-start.1 = (bf16[192,256]{1,0:T(8,128)(2,1)S(1)}, bf16[192,256]{1,0:T(8,128)(2,1)S(1)}, u32[]{:S(2)}, u32[]{:S(2)}) collective-permute-start(bf16[192,256]{1,0:T(8,128)(2,1)S(1)} %get-tuple-element.28), channel_id=1, source_target_pairs={{0,32},{1,46},{2,50},{3,60},{4,36},{5,42},{6,54},{7,56},{8,33},{9,... | collective-permute-start | bytes 294920 | tf_op jit(solution)/shard_map/ppermute | solution.py:268
  12.7 10.9 %collective-permute-start.2 = (bf16[192,256]{1,0:T(8,128)(2,1)S(1)}, bf16[192,256]{1,0:T(8,128)(2,1)S(1)}, u32[]{:S(2)}, u32[]{:S(2)}) collective-permute-start(bf16[192,256]{1,0:T(8,128)(2,1)S(1)} %get-tuple-element.29), channel_id=1, source_target_pairs={{0,64},{1,78},{2,82},{3,92},{4,68},{5,74},{6,86},{7,88},{8,65},{9,... | collective-permute-start | bytes 294920 | tf_op jit(solution)/shard_map/ppermute | solution.py:268
  23.6 5.5 %collective-permute-start.3 = (bf16[192,256]{1,0:T(8,128)(2,1)S(1)}, bf16[192,256]{1,0:T(8,128)(2,1)S(1)}, u32[]{:S(2)}, u32[]{:S(2)}) collective-permute-start(bf16[192,256]{1,0:T(8,128)(2,1)S(1)} %get-tuple-element.30), channel_id=1, source_target_pairs={{0,96},{1,110},{2,114},{3,124},{4,100},{5,106},{6,118},{7,120},{8,... | collective-permute-start | bytes 294920 | tf_op jit(solution)/shard_map/ppermute | solution.py:268
  29.1 0.9 copy-done
  30.0 0.9 copy-done.4
  30.9 0.9 copy-done.5
  31.9 0.8 fresh_layout.1
  32.7 4.0 %collective-permute-done.3 = bf16[192,256]{1,0:T(8,128)(2,1)S(1)} collective-permute-done((bf16[192,256]{1,0:T(8,128)(2,1)S(1)}, bf16[192,256]{1,0:T(8,128)(2,1)S(1)}, u32[]{:S(2)}, u32[]{:S(2)}) %collective-permute-start.3) | collective-permute-done | bytes 98336 | tf_op jit(solution)/shard_map/ppermute | solution.py:268
  36.8 12.2 %collective-permute-start.5 = (bf16[960,256]{1,0:T(8,128)(2,1)S(1)}, bf16[960,256]{1,0:T(8,128)(2,1)S(1)}, u32[]{:S(2)}, u32[]{:S(2)}) collective-permute-start(bf16[960,256]{1,0:T(8,128)(2,1)S(1)} %constant_dynamic-update-slice_fusion.refs_0_), channel_id=1, source_target_pairs={{0,6},{2,4},{4,2},{6,0},{1,7},{3,5},{5,3},{7,1},{8,14},{10,12},{12... | collective-permute-start | bytes 1474568 | tf_op jit(solution)/shard_map/ppermute | solution.py:282
  48.9 2.7 %collective-permute-start.4 = (bf16[960,256]{1,0:T(8,128)(2,1)S(1)}, bf16[960,256]{1,0:T(8,128)(2,1)S(1)}, u32[]{:S(2)}, u32[]{:S(2)}) collective-permute-start(bf16[960,256]{1,0:T(8,128)(2,1)S(1)} %constant_dynamic-update-slice_fusion.refs_0_), channel_id=1, source_target_pairs={{0,2},{2,0},{4,6},{6,4},{1,3},{3,1},{5,7},{7,5},{8,10},{10,8},{12,... | collective-permute-start | bytes 1474568 | tf_op jit(solution)/shard_map/ppermute | solution.py:282
  51.6 10.9 %all-to-all-start = ((bf16[16,96,128]{2,1,0:T(8,128)(2,1)}), bf16[16,96,128]{2,1,0:T(8,128)(2,1)S(1)}, u32[]{:S(2)}, u32[]{:S(2)}) async-start(bf16[16,96,128]{2,1,0:T(8,128)(2,1)} %get-tuple-element.32), calls=%async_computation | async-start | bytes 786432 | tf_op jit(solution)/shard_map/all_to_all | solution.py:277
  62.5 1.9 %collective-permute-start.8 = (bf16[960,256]{1,0:T(8,128)(2,1)S(1)}, bf16[960,256]{1,0:T(8,128)(2,1)}, u32[]{:S(2)}, u32[]{:S(2)}) collective-permute-start(bf16[960,256]{1,0:T(8,128)(2,1)S(1)} %constant_dynamic-update-slice_fusion.refs_0_), channel_id=1, source_target_pairs={{0,4},{2,6},{4,0},{6,2},{1,5},{3,7},{5,1},{7,3},{8,12},{10,14},{12... | collective-permute-start | bytes 1474568 | tf_op jit(solution)/shard_map/ppermute | solution.py:282
  64.4 6.4 %collective-permute-done.5.refs_5_ = bf16[960,256]{1,0:T(8,128)(2,1)S(1)} collective-permute-done((bf16[960,256]{1,0:T(8,128)(2,1)S(1)}, bf16[960,256]{1,0:T(8,128)(2,1)S(1)}, u32[]{:S(2)}, u32[]{:S(2)}) %collective-permute-start.5) | collective-permute-done | bytes 491552 | tf_op jit(solution)/shard_map/ppermute | solution.py:282
  70.9 1.0 pad_maximum_fusion
  71.9 1.9 %collective-permute-start.6 = (bf16[1920,256]{1,0:T(8,128)(2,1)}, bf16[1920,256]{1,0:T(8,128)(2,1)S(1)}, u32[]{:S(2)}, u32[]{:S(2)}) collective-permute-start(bf16[1920,256]{1,0:T(8,128)(2,1)} %pad_maximum_fusion), channel_id=1, source_target_pairs={{0,1},{1,0},{2,3},{3,2},{4,5},{5,4},{6,7},{7,6},{8,9},{9,8},{10,11... | collective-permute-start | bytes 2949128 | tf_op jit(solution)/shard_map/ppermute | solution.py:286
  73.8 2.4 %collective-permute-start.7 = (bf16[960,256]{1,0:T(8,128)(2,1)S(1)}, bf16[960,256]{1,0:T(8,128)(2,1)}, u32[]{:S(2)}, u32[]{:S(2)}) collective-permute-start(bf16[960,256]{1,0:T(8,128)(2,1)S(1)} %constant_dynamic-update-slice_fusion.refs_0_), channel_id=1, source_target_pairs={{0,1},{1,0},{2,3},{3,2},{4,5},{5,4},{6,7},{7,6},{8,9},{9,8},{10,11... | collective-permute-start | bytes 1474568 | tf_op jit(solution)/shard_map/ppermute | solution.py:284
  76.2 1.9 %collective-permute-start.9 = (bf16[960,256]{1,0:T(8,128)(2,1)}, bf16[960,256]{1,0:T(8,128)(2,1)}, u32[]{:S(2)}, u32[]{:S(2)}) collective-permute-start(bf16[960,256]{1,0:T(8,128)(2,1)} %collective-permute-done.8.refs_2_), channel_id=1, source_target_pairs={{0,1},{1,0},{2,3},{3,2},{4,5},{5,4},{6,7},{7,6},{8,9},{9,8},{10,11... | collective-permute-start | bytes 1474568 | tf_op jit(solution)/shard_map/ppermute | solution.py:285
  78.5 1.8 %collective-permute-done.9.refs_3_ = bf16[960,256]{1,0:T(8,128)(2,1)} collective-permute-done((bf16[960,256]{1,0:T(8,128)(2,1)}, bf16[960,256]{1,0:T(8,128)(2,1)}, u32[]{:S(2)}, u32[]{:S(2)}) %collective-permute-start.9) | collective-permute-done | bytes 491552 | tf_op jit(solution)/shard_map/ppermute | solution.py:285
  80.3 0.8 all-to-all-done.q_ref
  81.2 6.7 %keys_first.1 = (f32[1,768]{1,0:T(1,128)S(1)}, f32[1,768]{1,0:T(1,128)S(1)}, f32[128,768]{1,0:T(8,128)S(1)}, f32[1,768]{1,0:T(1,128)S(1)}, f32[1,768]{1,0:T(1,128)S(1)}, /*index=5*/f32[128,768]{1,0:T(8,128)S(1)}) custom-call(s32[32]{0:T(128)S(1)} %stack.131.spans_ref, bf16[16,96,128]{2,1,0:T(8,128)(2,1)S(1)} %all-to-all-done.q_ref, ...), custom_call_target="tpu_custom_call" | custom-call | tf_op jit(solution)/shard_map/keys_first/pallas_call | solution.py:171
  87.8 4.4 %keys_last.1 = bf16[16,112,128]{2,1,0:T(8,128)(2,1)} custom-call(s32[32]{0:T(128)S(1)} %stack.131.spans_ref, bf16[16,96,128]{2,1,0:T(8,128)(2,1)S(1)} %all-to-all-done.q_ref, bf16[1920,256]{1,0:T(8,128)(2,1)S(1)} %collective-permute-done.6.refs_0_, f32[1,768]{1,0:T(1,128)S(1)} %get-tuple-element.37.refs_1_, f32[1,768]{1,0:T(1,128)S(1)} %get-tuple-element.38.refs_2_, ...), custom_call_target="tpu_custom_call" | custom-call | tf_op jit(solution)/shard_map/keys_last/pallas_call | solution.py:171
  92.2 8.3 %all-to-all-start.1 = ((bf16[16,112,128]{2,1,0:T(8,128)(2,1)}), bf16[16,112,128]{2,1,0:T(8,128)(2,1)S(1)}, u32[]{:S(2)}, u32[]{:S(2)}) async-start(bf16[16,112,128]{2,1,0:T(8,128)(2,1)} %keys_last.1), calls=%async_computation.1 | async-start | bytes 917504 | tf_op jit(solution)/shard_map/all_to_all | solution.py:316
  100.5 3.2 %collective-permute-start.10 = (bf16[48,5120]{1,0:T(8,128)(2,1)S(1)}, bf16[48,5120]{1,0:T(8,128)(2,1)S(1)}, u32[]{:S(2)}, u32[]{:S(2)}) collective-permute-start(bf16[48,5120]{1,0:T(8,128)(2,1)S(1)} %get-tuple-element.44), channel_id=1, source_target_pairs={{0,2},{2,0},{1,3},{3,1},{4,6},{6,4},{5,7},{7,5},{8,10},{10,8},{9,1... | collective-permute-start | bytes 1474568 | tf_op jit(solution)/shard_map/ppermute | solution.py:315
  103.8 13.3 %collective-permute-done.10 = bf16[48,5120]{1,0:T(8,128)(2,1)S(1)} collective-permute-done((bf16[48,5120]{1,0:T(8,128)(2,1)S(1)}, bf16[48,5120]{1,0:T(8,128)(2,1)S(1)}, u32[]{:S(2)}, u32[]{:S(2)}) %collective-permute-start.10) | collective-permute-done | bytes 491552 | tf_op jit(solution)/shard_map/ppermute | solution.py:315
  117.1 1.9 %collective-permute-start.11 = (bf16[96,5120]{1,0:T(8,128)(2,1)S(1)}, bf16[96,5120]{1,0:T(8,128)(2,1)S(1)}, u32[]{:S(2)}, u32[]{:S(2)}) collective-permute-start(bf16[96,5120]{1,0:T(8,128)(2,1)S(1)} %constant_dynamic-update-slice_fusion.4.near_ref), channel_id=1, source_target_pairs={{0,1},{1,0},{2,3},{3,2},{4,5},{5,4},{6,7},{7,6},{8,9},{9,8},{10,11... | collective-permute-start | bytes 2949128 | tf_op jit(solution)/shard_map/ppermute | solution.py:324
  119.0 2.5 %collective-permute-done.11.far_ref = bf16[96,5120]{1,0:T(8,128)(2,1)S(1)} collective-permute-done((bf16[96,5120]{1,0:T(8,128)(2,1)S(1)}, bf16[96,5120]{1,0:T(8,128)(2,1)S(1)}, u32[]{:S(2)}, u32[]{:S(2)}) %collective-permute-start.11) | collective-permute-done | bytes 983072 | tf_op jit(solution)/shard_map/ppermute | solution.py:324
  121.6 1.2 own_patch.1
  122.8 4.7 %all-to-all-done.1.both_ref = bf16[16,112,128]{2,1,0:T(8,128)(2,1)S(1)} async-done(((bf16[16,112,128]{2,1,0:T(8,128)(2,1)}), bf16[16,112,128]{2,1,0:T(8,128)(2,1)S(1)}, u32[]{:S(2)}, u32[]{:S(2)}) %all-to-all-start.1) | async-done | bytes 458784 | tf_op jit(solution)/shard_map/all_to_all | solution.py:316
  127.5 1.4 %merge.1 = bf16[48,2560]{1,0:T(8,128)(2,1)} custom-call(bf16[16,112,128]{2,1,0:T(8,128)(2,1)S(1)} %all-to-all-done.1.both_ref, f32[48,2560]{1,0:T(8,128)S(1)} %get-tuple-element.45.fresh_ref, f32[48,128]{1,0:T(8,128)S(1)} %get-tuple-element.46.fresh_log_ref), custom_call_target="tpu_custom_call" | custom-call | tf_op jit(solution)/shard_map/merge/pallas_call | solution.py:326
  (24 shorter events, 1.2 us)
Async XLA Ops:
  0.0 0.9 copy-start.2
  0.9 0.9 copy-start.3
  1.9 0.7 copy-start.6
  2.9 33.8 %collective-permute-start = (bf16[384,256]{1,0:T(8,128)(2,1)S(1)}, bf16[384,256]{1,0:T(8,128)(2,1)S(1)}, u32[]{:S(2)}, u32[]{:S(2)}) collective-permute-start(bf16[384,256]{1,0:T(8,128)(2,1)S(1)} %get-tuple-element.27), channel_id=1, source_target_pairs={{0,0},{1,14},{2,18},{3,28},{4,4},{5,10},{6,22},{7,24},{8,1},{9,15}... | collective-permute-start | bytes 589832 | tf_op jit(solution)/shard_map/ppermute | solution.py:268
  3.5 29.2 %collective-permute-start.1 = (bf16[192,256]{1,0:T(8,128)(2,1)S(1)}, bf16[192,256]{1,0:T(8,128)(2,1)S(1)}, u32[]{:S(2)}, u32[]{:S(2)}) collective-permute-start(bf16[192,256]{1,0:T(8,128)(2,1)S(1)} %get-tuple-element.28), channel_id=1, source_target_pairs={{0,32},{1,46},{2,50},{3,60},{4,36},{5,42},{6,54},{7,56},{8,33},{9,... | collective-permute-start | bytes 294920 | tf_op jit(solution)/shard_map/ppermute | solution.py:268
  12.7 20.1 %collective-permute-start.2 = (bf16[192,256]{1,0:T(8,128)(2,1)S(1)}, bf16[192,256]{1,0:T(8,128)(2,1)S(1)}, u32[]{:S(2)}, u32[]{:S(2)}) collective-permute-start(bf16[192,256]{1,0:T(8,128)(2,1)S(1)} %get-tuple-element.29), channel_id=1, source_target_pairs={{0,64},{1,78},{2,82},{3,92},{4,68},{5,74},{6,86},{7,88},{8,65},{9,... | collective-permute-start | bytes 294920 | tf_op jit(solution)/shard_map/ppermute | solution.py:268
  23.6 13.1 %collective-permute-start.3 = (bf16[192,256]{1,0:T(8,128)(2,1)S(1)}, bf16[192,256]{1,0:T(8,128)(2,1)S(1)}, u32[]{:S(2)}, u32[]{:S(2)}) collective-permute-start(bf16[192,256]{1,0:T(8,128)(2,1)S(1)} %get-tuple-element.30), channel_id=1, source_target_pairs={{0,96},{1,110},{2,114},{3,124},{4,100},{5,106},{6,118},{7,120},{8,... | collective-permute-start | bytes 294920 | tf_op jit(solution)/shard_map/ppermute | solution.py:268
  29.0 0.9 copy-start
  30.0 0.9 copy-start.4
  30.9 0.9 copy-start.5
  36.8 34.1 %collective-permute-start.5 = (bf16[960,256]{1,0:T(8,128)(2,1)S(1)}, bf16[960,256]{1,0:T(8,128)(2,1)S(1)}, u32[]{:S(2)}, u32[]{:S(2)}) collective-permute-start(bf16[960,256]{1,0:T(8,128)(2,1)S(1)} %constant_dynamic-update-slice_fusion.refs_0_), channel_id=1, source_target_pairs={{0,6},{2,4},{4,2},{6,0},{1,7},{3,5},{5,3},{7,1},{8,14},{10,12},{12... | collective-permute-start | bytes 1474568 | tf_op jit(solution)/shard_map/ppermute | solution.py:282
  48.9 21.9 %collective-permute-start.4 = (bf16[960,256]{1,0:T(8,128)(2,1)S(1)}, bf16[960,256]{1,0:T(8,128)(2,1)S(1)}, u32[]{:S(2)}, u32[]{:S(2)}) collective-permute-start(bf16[960,256]{1,0:T(8,128)(2,1)S(1)} %constant_dynamic-update-slice_fusion.refs_0_), channel_id=1, source_target_pairs={{0,2},{2,0},{4,6},{6,4},{1,3},{3,1},{5,7},{7,5},{8,10},{10,8},{12,... | collective-permute-start | bytes 1474568 | tf_op jit(solution)/shard_map/ppermute | solution.py:282
  51.6 29.6 %all-to-all-start = ((bf16[16,96,128]{2,1,0:T(8,128)(2,1)}), bf16[16,96,128]{2,1,0:T(8,128)(2,1)S(1)}, u32[]{:S(2)}, u32[]{:S(2)}) async-start(bf16[16,96,128]{2,1,0:T(8,128)(2,1)} %get-tuple-element.32), calls=%async_computation | async-start | bytes 786432 | tf_op jit(solution)/shard_map/all_to_all | solution.py:277
  62.5 13.7 %collective-permute-start.8 = (bf16[960,256]{1,0:T(8,128)(2,1)S(1)}, bf16[960,256]{1,0:T(8,128)(2,1)}, u32[]{:S(2)}, u32[]{:S(2)}) collective-permute-start(bf16[960,256]{1,0:T(8,128)(2,1)S(1)} %constant_dynamic-update-slice_fusion.refs_0_), channel_id=1, source_target_pairs={{0,4},{2,6},{4,0},{6,2},{1,5},{3,7},{5,1},{7,3},{8,12},{10,14},{12... | collective-permute-start | bytes 1474568 | tf_op jit(solution)/shard_map/ppermute | solution.py:282
  71.9 15.9 %collective-permute-start.6 = (bf16[1920,256]{1,0:T(8,128)(2,1)}, bf16[1920,256]{1,0:T(8,128)(2,1)S(1)}, u32[]{:S(2)}, u32[]{:S(2)}) collective-permute-start(bf16[1920,256]{1,0:T(8,128)(2,1)} %pad_maximum_fusion), channel_id=1, source_target_pairs={{0,1},{1,0},{2,3},{3,2},{4,5},{5,4},{6,7},{7,6},{8,9},{9,8},{10,11... | collective-permute-start | bytes 2949128 | tf_op jit(solution)/shard_map/ppermute | solution.py:286
  73.8 4.7 %collective-permute-start.7 = (bf16[960,256]{1,0:T(8,128)(2,1)S(1)}, bf16[960,256]{1,0:T(8,128)(2,1)}, u32[]{:S(2)}, u32[]{:S(2)}) collective-permute-start(bf16[960,256]{1,0:T(8,128)(2,1)S(1)} %constant_dynamic-update-slice_fusion.refs_0_), channel_id=1, source_target_pairs={{0,1},{1,0},{2,3},{3,2},{4,5},{5,4},{6,7},{7,6},{8,9},{9,8},{10,11... | collective-permute-start | bytes 1474568 | tf_op jit(solution)/shard_map/ppermute | solution.py:284
  76.2 4.1 %collective-permute-start.9 = (bf16[960,256]{1,0:T(8,128)(2,1)}, bf16[960,256]{1,0:T(8,128)(2,1)}, u32[]{:S(2)}, u32[]{:S(2)}) collective-permute-start(bf16[960,256]{1,0:T(8,128)(2,1)} %collective-permute-done.8.refs_2_), channel_id=1, source_target_pairs={{0,1},{1,0},{2,3},{3,2},{4,5},{5,4},{6,7},{7,6},{8,9},{9,8},{10,11... | collective-permute-start | bytes 1474568 | tf_op jit(solution)/shard_map/ppermute | solution.py:285
  92.2 35.3 %all-to-all-start.1 = ((bf16[16,112,128]{2,1,0:T(8,128)(2,1)}), bf16[16,112,128]{2,1,0:T(8,128)(2,1)S(1)}, u32[]{:S(2)}, u32[]{:S(2)}) async-start(bf16[16,112,128]{2,1,0:T(8,128)(2,1)} %keys_last.1), calls=%async_computation.1 | async-start | bytes 917504 | tf_op jit(solution)/shard_map/all_to_all | solution.py:316
  100.5 21.0 %copy-start.1 = (bf16[48,2560]{1,0:T(8,128)(2,1)S(1)}, bf16[48,2560]{1,0:T(8,128)(2,1)}, u32[]{:S(2)}) copy-start(bf16[48,2560]{1,0:T(8,128)(2,1)} %q_ref.3) | copy-start | bytes 737284
  100.5 16.5 %collective-permute-start.10 = (bf16[48,5120]{1,0:T(8,128)(2,1)S(1)}, bf16[48,5120]{1,0:T(8,128)(2,1)S(1)}, u32[]{:S(2)}, u32[]{:S(2)}) collective-permute-start(bf16[48,5120]{1,0:T(8,128)(2,1)S(1)} %get-tuple-element.44), channel_id=1, source_target_pairs={{0,2},{2,0},{1,3},{3,1},{4,6},{6,4},{5,7},{7,5},{8,10},{10,8},{9,1... | collective-permute-start | bytes 1474568 | tf_op jit(solution)/shard_map/ppermute | solution.py:315
  117.1 4.5 %collective-permute-start.11 = (bf16[96,5120]{1,0:T(8,128)(2,1)S(1)}, bf16[96,5120]{1,0:T(8,128)(2,1)S(1)}, u32[]{:S(2)}, u32[]{:S(2)}) collective-permute-start(bf16[96,5120]{1,0:T(8,128)(2,1)S(1)} %constant_dynamic-update-slice_fusion.4.near_ref), channel_id=1, source_target_pairs={{0,1},{1,0},{2,3},{3,2},{4,5},{5,4},{6,7},{7,6},{8,9},{9,8},{10,11... | collective-permute-start | bytes 2949128 | tf_op jit(solution)/shard_map/ppermute | solution.py:324
